TPU v7x, 128 devices: a whole 4x4x4 slice. The times are simulated.
128 devices in a mesh: dp: 32 (over z, y, x_hi), mp: 4 (over x_lo, core).
Axes of the slice: x: 4 (x_hi: 2, x_lo: 2; x = x_hi * 2 + x_lo), y: 4, z: 4, core: 2. Of those that a mesh axis runs over, the one named last changes fastest.
Arguments:
- train_acts: bfloat16 [128, 64, 4096], P('dp', None, 'mp')
- train_grads: bfloat16 [128, 64, 14336], P('dp', None, 'mp'), may hold values from -6 to 6
- train_lengths: int32 [128], P('dp'), may hold values from 1 to 64, as said below
- query_acts: bfloat16 [64, 8, 4096], P('dp', None, 'mp'), may hold values from -6 to 6
- query_grads: bfloat16 [64, 8, 14336], P('dp', None, 'mp'), may hold values from -6 to 6
- query_lengths: int32 [64], P('dp'), may hold values from 4 to 8, as said below
- proj_in: bfloat16 [64, 4096], P(None, 'mp'), may hold values from -0.09375 to 0.09375
- proj_out: bfloat16 [64, 14336], P(None, 'mp'), may hold values from -0.046875 to 0.046875
Outputs:
- precond: float32 [64, 4096], P(None, 'mp')
- scores: float32 [128, 64], P('dp', 'mp')
Inputs may be any that keep to these rules, and one draw needn't show every extreme that they name: `train_lengths`: each training row uses at least one slot; some row uses all 64. `query_lengths`: some query uses all 8 slots and some uses exactly half of them.
All inputs are finite; a program needn't handle non-finite values.
Results may differ from a plain program's by a relative error of at most 0.0006.
Values sent between devices are 32-bit elements; how exact they have to be, the bound alone decides.
No kernel may reach another device: no remote copies, remote signals or barrier semaphores. Data moves between devices by JAX's collectives and lax.ppermute only.
A program may use at most 64 MiB of HBM per device.

v0:
```python
import math

import jax
import jax.numpy as jnp
from jax import lax
from jax.sharding import PartitionSpec as P

ITERS = 4


damping = 0.5
epsilon = 1e-06


def project(values, weights):
    return lax.dot_general(
        values, weights, (((2,), (1,)), ((), ())), preferred_element_type=jnp.float32
    )


def squared_norms(values):
    return lax.psum(jnp.sum(values * values, axis=1), "mp")


def spread_back(row_values, features):
    return lax.psum(jnp.dot(row_values.T, features, precision=lax.Precision.HIGHEST), "dp")


def local(
    train_acts,
    train_grads,
    train_lengths,
    query_acts,
    query_grads,
    query_lengths,
    proj_in,
    proj_out,
):
    highest = lax.Precision.HIGHEST
    rows_dev, length, _ = train_acts.shape
    query_rows, query_slots, _ = query_acts.shape
    rank = proj_in.shape[0]
    half_rank = rank // lax.axis_size("mp")
    data_size = lax.axis_size("dp")
    total_rows = rows_dev * data_size
    train_in = project(train_acts, proj_in)
    train_out = project(train_grads, proj_out)
    query_in = project(query_acts, proj_in)
    query_out = project(query_grads, proj_out)
    train_in, train_out, query_in, query_out = lax.psum(
        (train_in, train_out, query_in, query_out), "mp"
    )
    offset = lax.axis_index("mp") * half_rank
    train_half = lax.dynamic_slice_in_dim(train_out, offset, half_rank, 2)
    query_half = lax.dynamic_slice_in_dim(query_out, offset, half_rank, 2)
    token_mask = (jnp.arange(length, dtype=jnp.int32)[None, :] < train_lengths[:, None]).astype(
        jnp.float32
    )
    features = jnp.einsum(
        "rti,rtj->rij", train_half * token_mask[:, :, None], train_in, precision=highest
    )
    features = features.reshape(rows_dev, half_rank * rank) / math.sqrt(length)
    query_mask = (
        jnp.arange(query_slots, dtype=jnp.int32)[None, :] < query_lengths[:, None]
    ).astype(jnp.float32)
    qlocal = jnp.einsum(
        "qti,qtj->qij", query_half * query_mask[:, :, None], query_in, precision=highest
    )
    qlocal = qlocal.reshape(query_rows, half_rank * rank) / math.sqrt(query_slots)
    trace_value = lax.psum(jnp.sum(features * features), ("dp", "mp"))
    damp_value = damping * trace_value / (total_rows * rank * rank) + epsilon
    qfeatures = lax.all_gather(qlocal, "dp", axis=0, tiled=True)
    solution = jnp.zeros_like(qfeatures)
    residual = qfeatures
    direction = qfeatures
    norm_now = squared_norms(residual)
    for step in range(ITERS):
        row_partial = jnp.dot(features, direction.T, precision=highest)
        row_values = lax.psum(row_partial, "mp")
        operator_image = damp_value * direction + spread_back(row_values, features) / total_rows
        curvature = lax.psum(jnp.sum(direction * operator_image, axis=1), "mp")
        step_size = norm_now / curvature
        solution = solution + step_size[:, None] * direction
        residual = residual - step_size[:, None] * operator_image
        norm_next = squared_norms(residual)
        direction = residual + (norm_next / norm_now)[:, None] * direction
        norm_now = norm_next
    score_partial = jnp.dot(features, solution.T, precision=highest)
    scores = lax.psum_scatter(score_partial, "mp", scatter_dimension=1, tiled=True)
    return (solution, scores)


def solution(mesh):
    in_specs = (
        P("dp", None, "mp"),
        P("dp", None, "mp"),
        P("dp"),
        P("dp", None, "mp"),
        P("dp", None, "mp"),
        P("dp"),
        P(None, "mp"),
        P(None, "mp"),
    )
    out_specs = (P(None, "mp"), P("dp", "mp"))
    return jax.shard_map(local, mesh=mesh, in_specs=in_specs, out_specs=out_specs, check_vma=False)
```

profile of v0, /device:TPU:1, one launch (start us, length us, event | category | flops | bytes accessed | tf_op | source)
XLA Modules:
  0.0 1621.0 jit_solution(13936238651618942642)
XLA Ops:
  7.3 2.2 fusion.4
  9.4 2.7 fusion
  12.7 10.5 all-reduce.1
  23.5 84.6 %all-gather = f32[32,2,1024]{2,1,0:T(2,128)S(1)} all-gather(f32[1,2,1024]{2,1,0:T(2,128)S(1)} %reshape.61), channel_id=1, replica_groups=mesh['dp'=32,'mp'=4] {'dp'}, dimensions={0}, use_global_device_ids=true | all-gather | bytes 270336 | tf_op jit(solution)/shard_map/all_gather | solution.py:72
  108.4 1.8 multiply_reduce_fusion.8
  110.5 20.9 %psum.153 = f32[4,64]{1,0:T(4,128)S(1)} all-reduce(f32[4,64]{1,0:T(4,128)S(1)} %fusion.19), channel_id=1, replica_groups=mesh['dp'=32,'mp'=4] {'mp'}, use_global_device_ids=true, to_apply=%region_8.0 | all-reduce | flops 256 | bytes 2048 | tf_op jit(solution)/shard_map/psum | solution.py:79
  131.3 1.1 fusion.20
  132.5 63.2 %psum.152 = f32[]{:T(128)} all-reduce(f32[]{:T(128)} %get-tuple-element.14), channel_id=1, replica_groups=mesh['dp'=32,'mp'=4] {'dp','mp'}, use_global_device_ids=true, to_apply=%region_7.0 | all-reduce | flops 1 | bytes 8 | tf_op jit(solution)/shard_map/psum | solution.py:70
  196.4 256.3 %all-reduce.9.cloned.1.call-done = f32[64,1024]{1,0:T(8,128)} async-done(((f32[64,1024]{1,0:T(8,128)}), f32[64,1024]{1,0:T(8,128)}) %all-reduce.9.cloned.1.call-update) | async-done | bytes 262160 | tf_op jit(solution)/shard_map/psum | solution.py:26
  452.8 1.2 multiply_reduce_fusion.6
  454.0 26.9 %all-reduce = (f32[64]{0:T(128)S(1)}, f32[64]{0:T(128)S(1)}) all-reduce(f32[64]{0:T(128)S(1)} %get-tuple-element.3, f32[64]{0:T(128)S(1)} %get-tuple-element.2), channel_id=1, replica_groups=mesh['dp'=32,'mp'=4] {'mp'}, use_global_device_ids=true, to_apply=%region_3.0 | all-reduce | flops 128 | bytes 1024 | tf_op jit(solution)/shard_map/psum | solution.py:22
  480.9 1.2 multiply_reduce_fusion.5
  482.1 5.8 psum.156
  487.8 1.3 fusion.18
  489.1 6.5 psum.157
  495.7 1.1 fusion.21
  496.9 327.5 %all-reduce.11.cloned.1.call-done = f32[64,1024]{1,0:T(8,128)} async-done(((f32[64,1024]{1,0:T(8,128)}), f32[64,1024]{1,0:T(8,128)}) %all-reduce.11.cloned.1.call-update) | async-done | bytes 262160 | tf_op jit(solution)/shard_map/psum | solution.py:26
  824.4 1.2 multiply_reduce_fusion.4
  825.6 26.9 %psum.159 = f32[64]{0:T(128)S(1)} all-reduce(f32[64]{0:T(128)S(1)} %multiply_reduce_fusion.4), channel_id=1, replica_groups=mesh['dp'=32,'mp'=4] {'mp'}, use_global_device_ids=true, to_apply=%region_17.0 | all-reduce | flops 64 | bytes 512 | tf_op jit(solution)/shard_map/psum | solution.py:81
  852.5 1.3 multiply_reduce_fusion.3
  853.8 5.8 psum.160
  860.0 6.5 psum.161
  867.7 327.5 %all-reduce.13.cloned.1.call-done = f32[64,1024]{1,0:T(8,128)} async-done(((f32[64,1024]{1,0:T(8,128)}), f32[64,1024]{1,0:T(8,128)}) %all-reduce.13.cloned.1.call-update) | async-done | bytes 262160 | tf_op jit(solution)/shard_map/psum | solution.py:26
  1196.3 26.9 %psum.163 = f32[64]{0:T(128)S(1)} all-reduce(f32[64]{0:T(128)S(1)} %multiply_reduce_fusion.2), channel_id=1, replica_groups=mesh['dp'=32,'mp'=4] {'mp'}, use_global_device_ids=true, to_apply=%region_23.0 | all-reduce | flops 64 | bytes 512 | tf_op jit(solution)/shard_map/psum | solution.py:81
  1223.3 1.2 multiply_reduce_fusion.1
  1224.4 5.8 psum.164
  1230.6 6.5 psum.165
  1238.3 327.5 %all-reduce.15.cloned.1.call-done = f32[64,1024]{1,0:T(8,128)} async-done(((f32[64,1024]{1,0:T(8,128)}), f32[64,1024]{1,0:T(8,128)}) %all-reduce.15.cloned.1.call-update) | async-done | bytes 262160 | tf_op jit(solution)/shard_map/psum | solution.py:26
  1565.8 1.2 multiply_reduce_fusion
  1567.0 26.9 %psum.167 = f32[64]{0:T(128)S(1)} all-reduce(f32[64]{0:T(128)S(1)} %multiply_reduce_fusion), channel_id=1, replica_groups=mesh['dp'=32,'mp'=4] {'mp'}, use_global_device_ids=true, to_apply=%region_29.0 | all-reduce | flops 64 | bytes 512 | tf_op jit(solution)/shard_map/psum | solution.py:81
  1595.1 17.7 %reduce-scatter.4.cloned.1.call-done = f32[16,4]{1,0:T(8,128)} async-done(((f32[64,4]{1,0:T(8,128)}), f32[16,4]{1,0:T(8,128)}) %reduce-scatter.4.cloned.1.call-update) | async-done | bytes 272
  1612.8 1.3 copy.11
  (55 shorter events, 7.1 us)
Async XLA Ops:
  7.2 2.3 copy-start
  7.2 5.1 copy-start.4
  7.2 5.2 copy-start.2
  7.2 5.0 copy-start.8
  7.2 5.1 copy-start.6
  7.2 5.2 copy-start.5
  7.2 101.1 %all-reduce.17.cloned.1.call-start = ((), (), s32[]{:S(2)}) async-start(), calls=%async_computation.6 | async-start | bytes 524288 | tf_op jit(solution)/shard_map/psum | solution.py:50
  9.4 98.8 %copy-start.7 = (s32[4]{0:T(128)S(1)}, s32[4]{0:T(128)}, u32[]{:S(2)}) copy-start(s32[4]{0:T(128)} %param.10) | copy-start | bytes 52
  12.1 440.6 %all-reduce.9.cloned.1.call-start = ((), (), s32[]{:S(2)}) async-start(), calls=%async_computation.1 | async-start | bytes 524288 | tf_op jit(solution)/shard_map/psum | solution.py:26
  132.5 691.9 %all-reduce.11.cloned.1.call-start = ((), (), s32[]{:S(2)}) async-start(), calls=%async_computation.2 | async-start | bytes 524288 | tf_op jit(solution)/shard_map/psum | solution.py:26
  452.8 371.6 %copy-start.1 = (f32[64,1024]{1,0:T(8,128)S(1)}, f32[64,1024]{1,0:T(8,128)}, u32[]{:S(2)}) copy-start(f32[64,1024]{1,0:T(8,128)} %all-reduce.9.cloned.1.call-done) | copy-start | bytes 786436
  496.8 698.4 %all-reduce.13.cloned.1.call-start = ((), (), s32[]{:S(2)}) async-start(), calls=%async_computation.3 | async-start | bytes 524288 | tf_op jit(solution)/shard_map/psum | solution.py:26
  867.7 698.1 %all-reduce.15.cloned.1.call-start = ((), (), s32[]{:S(2)}) async-start(), calls=%async_computation.4 | async-start | bytes 524288 | tf_op jit(solution)/shard_map/psum | solution.py:26
  1238.2 374.6 %reduce-scatter.4.cloned.1.call-start = ((), (), s32[]{:S(2)}) async-start(), calls=%async_computation.5 | async-start | bytes 40960
  1594.2 20.0 %copy-start.3 = (f32[64,1024]{1,0:T(8,128)}, f32[64,1024]{1,0:T(8,128)S(1)}, u32[]{:S(2)}) copy-start(f32[64,1024]{1,0:T(8,128)S(1)} %multiply_add_fusion) | copy-start | bytes 786436
Sparse Core Ops, SparseCore 0:
  12.3 40.4 all-reduce.16
  132.6 320.1 all-reduce.8
  496.9 327.3 all-reduce.10
  867.8 327.3 all-reduce.12
  1238.4 327.3 all-reduce.14
  1595.3 17.5 reduce-scatter.3
where the time goes:
time: 1620 us
  waiting for transfers between devices  1260 us (78%)
  blocking collectives  324 us (20%)
    psum x4, waiting for transfers between devices, spread_back(): lax.psum(jnp.dot(row_values.T, features, precision=lax.Precision.HIGHEST)...  1240 us
    all_gather x1, blocking collectives, local(): qfeatures = lax.all_gather(qlocal, 'dp', axis=0, tiled=True)  84.6 us
    psum x3, blocking collectives, local(): curvature = lax.psum(jnp.sum(direction * operator_image, axis=1), 'mp')  80.8 us
    psum x1, blocking collectives, local(): trace_value = lax.psum(jnp.sum(features * features), ('dp', 'mp'))  63.2 us
    psum x4, blocking collectives, squared_norms(): return lax.psum(jnp.sum(values * values, axis=1), 'mp')  44.2 us
    psum x4, blocking collectives, local(): row_values = lax.psum(row_partial, 'mp')  40.4 us
  transfers between devices with their start and end apart: 6, of which 5 were waited for; matrix products, arithmetic and copies ran while one was open for 0% of the time, Pallas kernels for 0%

commit v1 on v0

v1 whole, which is shorter than its diff:
```python
import math

import jax
import jax.numpy as jnp
from jax import lax
from jax.experimental import pallas as pl
from jax.experimental.pallas import tpu as pltpu
from jax.sharding import PartitionSpec as P

ITERS = 4
DAMPING = 0.5
EPSILON = 1e-06
VMEM = 48 * 2**20
NZ, NY, NX = 4, 4, 2

NT = (((1,), (1,)), ((), ()))
NN = (((1,), (0,)), ((), ()))
TN = (((0,), (0,)), ((), ()))


def dot(a, b, dims):
    return lax.dot_general(
        a, b, dims, precision=lax.Precision.HIGHEST, preferred_element_type=jnp.float32
    )


def project_kernel(ta, tg, qa, qg, pi, po, own, to1, to2, to3,
                   ta_v, tg_v, qa_v, qg_v, pi_v, po_v, out_t, sems):
    copies = []
    for i, (src, dst) in enumerate(((pi, pi_v), (ta, ta_v), (qa, qa_v), (po, po_v), (qg, qg_v))):
        copies.append(pltpu.make_async_copy(src, dst, sems.at[i]))
    rows = tg.shape[0]
    for r in range(rows):
        copies.append(pltpu.make_async_copy(tg.at[r], tg_v.at[r], sems.at[5 + r]))
    for c in copies:
        c.start()
    me = lax.axis_index("mp")
    outs = (own, to1, to2, to3)

    def mm(a, b):
        return lax.dot_general(a, b, NT, preferred_element_type=jnp.float32)

    copies[0].wait()
    copies[1].wait()
    copies[2].wait()
    weights = pi_v[...]
    train_in = mm(ta_v[...].reshape(-1, ta_v.shape[2]), weights).T
    query_in = mm(qa_v[...], weights)
    for o in outs:
        o[0:64, :] = train_in[:, 0:128]
        o[80:144, :] = train_in[:, 128:256]
    copies[3].wait()
    copies[4].wait()
    weights = po_v[...]
    query_out = mm(qg_v[...], weights)
    queries = jnp.concatenate([query_in, query_out], axis=1)
    for o in outs:
        o[160:176, :] = queries
    for r in range(0, rows, 2):
        copies[5 + r].wait()
        copies[6 + r].wait()
        pair = mm(tg_v[r : r + 2].reshape(-1, tg_v.shape[2]), weights).T
        out_t[:, 64 * r : 64 * r + 128] = pair
    for k, o in enumerate(outs):
        quarter = out_t[pl.ds(pl.multiple_of((me ^ k) * 16, 16), 16), :]
        o[64:80, :] = quarter[:, 0:128]
        o[144:160, :] = quarter[:, 128:256]


def features_kernel(tl, ql, p0, p1, p2, p3, feats, scr, qscr):
    me = lax.axis_index("mp")
    x = (p0[...] + p1[...]) + (p2[...] + p3[...])
    lane = lax.broadcasted_iota(jnp.int32, (16, 128), 1)
    low = lax.broadcasted_iota(jnp.int32, (8, 128), 1) < 64
    for pair in range(2):
        base = 80 * pair
        inn = x[base : base + 64]
        out = x[base + 64 : base + 80]
        first = jnp.where(lane < tl[2 * pair], jnp.where(lane < 64, out, 0.0), 0.0)
        second = jnp.where(lane < 64 + tl[2 * pair + 1], jnp.where(lane >= 64, out, 0.0), 0.0)
        left = jnp.concatenate([first, second], axis=0)
        right = jnp.concatenate([inn, inn], axis=0)
        scr[32 * pair : 32 * pair + 32, :] = dot(left, right, NT)
    for r in range(4):
        even = scr[pl.ds(16 * r, 8, stride=2), :]
        odd = scr[pl.ds(16 * r + 1, 8, stride=2), :]
        feats[8 * r : 8 * r + 8, :] = jnp.where(low, even, odd) * 0.125
    q = x[160:176]
    slot = lax.broadcasted_iota(jnp.int32, (16, 64), 0)
    qin = q[:, 0:64]
    qout = q[:, 64:128]
    right = jnp.concatenate([qin, qin], axis=1)
    for r in range(2):
        keep = (slot >= 8 * r) & (slot < 8 * r + ql[r])
        qscr[64 * r : 64 * r + 64, :] = dot(jnp.where(keep, qout, 0.0), right, TN)
    for r in range(2):
        scr[0:16, :] = qscr[pl.ds(pl.multiple_of(64 * r + me * 16, 16), 16), :]
        even = scr[pl.ds(0, 8, stride=2), :]
        odd = scr[pl.ds(1, 8, stride=2), :]
        feats[32 + 8 * r : 40 + 8 * r, :] = jnp.where(low, even, odd) * (1.0 / math.sqrt(8.0))


def gram_kernel(y0, y1, y2, y3, part, fq, fs, qs):
    dp = lax.axis_index("dp")
    mz, my, mx = dp // (NY * NX), (dp // NX) % NY, dp % NX
    for j, ref in enumerate((y0, y1, y2, y3)):
        for k in range(NZ):
            for e in range(NX):
                slot = ((mz + NZ - k) % NZ * NY + (my + NY - j) % NY) * NX + (mx ^ e)
                at = 48 * (2 * k + e)
                fs[pl.ds(pl.multiple_of(slot * 32, 32), 32), :] = ref[at : at + 32, :]
                qs[pl.ds(pl.multiple_of(slot * 16, 16), 16), :] = ref[at + 32 : at + 48, :]
    total = jnp.zeros((192, 128), jnp.float32)
    squares = jnp.zeros((64, 128), jnp.float32)
    for a in range(8):
        f = fs[pl.ds(a, 128, stride=8), :]
        q = qs[pl.ds(a, 64, stride=8), :]
        fq[a, 0:128, :] = f
        fq[a, 128:192, :] = q
        total += dot(jnp.concatenate([f, q], axis=0), f, NT)
        squares += q * q
    part[0:192, :] = total
    norms = dot(jnp.ones((8, 128), jnp.float32), squares, NT)
    part[192:200, :] = jnp.concatenate([norms, norms], axis=1)


def solve_kernel(p0, p1, p2, p3, fq, precond, scores, ys):
    dp = lax.axis_index("dp")
    me = lax.axis_index("mp")
    x = (p0[...] + p1[...]) + (p2[...] + p3[...])
    gram = x[0:128]
    cross = x[128:192]
    row = lax.broadcasted_iota(jnp.int32, (64, 128), 0)
    col = lax.broadcasted_iota(jnp.int32, (64, 128), 1)
    norm_q = jnp.sum(jnp.where(row == col, jnp.broadcast_to(x[192:193], (64, 128)), 0.0),
                     axis=1, keepdims=True)
    grow = lax.broadcasted_iota(jnp.int32, (128, 128), 0)
    gcol = lax.broadcasted_iota(jnp.int32, (128, 128), 1)
    trace = jnp.sum(jnp.where(grow == gcol, gram, 0.0))
    damp = DAMPING * trace / (128 * 64 * 64) + EPSILON
    inv_rows = 1.0 / 128

    def inner(alpha, w, y):
        return alpha * (alpha * norm_q + jnp.sum(cross * w, axis=1, keepdims=True)) + jnp.sum(
            w * y, axis=1, keepdims=True
        )

    ra, rw, ry = jnp.ones((64, 1), jnp.float32), jnp.zeros((64, 128), jnp.float32), cross
    da, dw, dy = ra, rw, ry
    za, zw, zy = jnp.zeros((64, 1), jnp.float32), rw, rw
    rr = norm_q
    dd = norm_q
    for step in range(ITERS):
        curvature = damp * dd + jnp.sum(dy * dy, axis=1, keepdims=True) * inv_rows
        size = rr / curvature
        za, zw, zy = za + size * da, zw + size * dw, zy + size * dy
        if step == ITERS - 1:
            break
        iy = damp * dy + dot(dy, gram, NN) * inv_rows
        ra = ra - size * (damp * da)
        rw = rw - size * (damp * dw + dy * inv_rows)
        ry = ry - size * iy
        new = inner(ra, rw, ry)
        ratio = new / rr
        da, dw, dy = ra + ratio * da, rw + ratio * dw, ry + ratio * dy
        rr = new
        dd = inner(da, dw, dy)
    for a in range(8):
        precond[:, 128 * a : 128 * a + 128] = za * fq[a, 128:192, :] + dot(zw, fq[a, 0:128, :], NN)
    ys[...] = zy
    mine = ys[pl.ds(pl.multiple_of(me * 16, 16), 16), :]
    pick = (lax.broadcasted_iota(jnp.int32, (8, 128), 1)
            == lax.broadcasted_iota(jnp.int32, (8, 128), 0) + 4 * dp).astype(jnp.float32)
    scores[...] = dot(pick, mine, NT)[0:4]


def whole(n):
    return [pl.BlockSpec(memory_space=pltpu.VMEM)] * n


def call(kernel, shapes, in_specs, scratch, name):
    return pl.pallas_call(
        kernel,
        out_shape=[jax.ShapeDtypeStruct(s, jnp.float32) for s in shapes],
        in_specs=in_specs,
        out_specs=whole(len(shapes)),
        scratch_shapes=scratch,
        compiler_params=pltpu.CompilerParams(vmem_limit_bytes=VMEM),
        name=name,
    )


def dp_index(z, y, x):
    return (z * NY + y) * NX + x


def shift(dz, dy, dx):
    return [
        (dp_index(z, y, x), dp_index((z + dz) % NZ, (y + dy) % NY, (x + dx) % NX))
        for z in range(NZ)
        for y in range(NY)
        for x in range(NX)
    ]


def local(train_acts, train_grads, train_lengths, query_acts, query_grads, query_lengths,
          proj_in, proj_out):
    d, ff = proj_in.shape[1], proj_out.shape[1]
    bf = jnp.bfloat16
    own, *others = call(
        project_kernel,
        [(176, 128)] * 4,
        [pl.BlockSpec(memory_space=pl.ANY)] * 6,
        [
            pltpu.VMEM((4, 64, d), bf),
            pltpu.VMEM((4, 64, ff), bf),
            pltpu.VMEM((16, d), bf),
            pltpu.VMEM((16, ff), bf),
            pltpu.VMEM((64, d), bf),
            pltpu.VMEM((64, ff), bf),
            pltpu.VMEM((64, 256), jnp.float32),
            pltpu.SemaphoreType.DMA((9,)),
        ],
        "project",
    )(train_acts, train_grads, query_acts.reshape(16, d), query_grads.reshape(16, ff),
      proj_in, proj_out)
    got = [
        lax.ppermute(o, "mp", [(i, i ^ k) for i in range(4)]) for k, o in zip((1, 2, 3), others)
    ]
    smem = pl.BlockSpec(memory_space=pltpu.SMEM)
    (tiles,) = call(
        features_kernel,
        [(48, 128)],
        [smem, smem] + whole(4),
        [pltpu.VMEM((64, 128), jnp.float32), pltpu.VMEM((128, 128), jnp.float32)],
        "features",
    )(train_lengths, query_lengths, own, *got)
    tiles = jnp.concatenate([tiles, lax.ppermute(tiles, "dp", shift(0, 0, 1))], axis=0)
    tiles = jnp.concatenate(
        [tiles] + [lax.ppermute(tiles, "dp", shift(k, 0, 0)) for k in range(1, NZ)], axis=0
    )
    planes = [tiles] + [lax.ppermute(tiles, "dp", shift(0, k, 0)) for k in range(1, NY)]
    part, fq = call(
        gram_kernel,
        [(200, 128), (8, 192, 128)],
        whole(4),
        [pltpu.VMEM((1024, 128), jnp.float32), pltpu.VMEM((512, 128), jnp.float32)],
        "gram",
    )(*planes)
    got = [lax.ppermute(part, "mp", [(i, i ^ k) for i in range(4)]) for k in (1, 2, 3)]
    precond, scores = call(
        solve_kernel,
        [(64, 1024), (4, 16)],
        whole(5),
        [pltpu.VMEM((64, 128), jnp.float32)],
        "solve",
    )(part, *got, fq)
    return precond, scores


def solution(mesh):
    in_specs = (
        P("dp", None, "mp"),
        P("dp", None, "mp"),
        P("dp"),
        P("dp", None, "mp"),
        P("dp", None, "mp"),
        P("dp"),
        P(None, "mp"),
        P(None, "mp"),
    )
    out_specs = (P(None, "mp"), P("dp", "mp"))
    return jax.shard_map(local, mesh=mesh, in_specs=in_specs, out_specs=out_specs, check_vma=False)
```

time: 1620 us -> 59 us (0.04)
  waiting for transfers between devices: 1260 us -> 25.2 us
  blocking collectives: 324 us -> 0 us
  starting transfers between devices: 0.25 us -> 18.2 us
    psum x5 -> x0, waiting for transfers between devices: 1240 us -> none  [the longest x4 1240 us: spread_back(): lax.psum(jnp.dot(row_values.T, features, precision=lax.Precision.HIGHEST)...]
    psum x13 -> x0, blocking collectives: 239 us -> none  [the longest x3 80.8 us: local(): curvature = lax.psum(jnp.sum(direction * operator_image, axis=1), 'mp')]
    all_gather x1 -> x0, blocking collectives: 84.6 us -> none  [local(): qfeatures = lax.all_gather(qlocal, 'dp', axis=0, tiled=True)]
    ppermute x0 -> x13, waiting for transfers between devices: none -> 25.2 us  [the longest x3 9.92 us: local(): lax.ppermute(tiles, 'dp', shift(0, k, 0))]
    ppermute x0 -> x13, starting transfers between devices: none -> 18.2 us  [the longest x3 4.54 us: local(): lax.ppermute(tiles, 'dp', shift(k, 0, 0))]
    unnamed x7 -> x0, waiting for transfers between devices: 17.8 us -> none
  transfers between devices with their start and end apart: 6 -> 13, of which waited for: 5 -> 9; matrix products, arithmetic and copies ran while one was open for 0% -> 0% of each run, Pallas kernels for 0% -> 0%
where the time goes in v1:
time: 59 us; the launch traced here: 58.7 us
  waiting for transfers between devices  25.2 us (43%)
  starting transfers between devices  18.2 us (31%)
  Pallas kernels  8.46 us (14%)
  local copies, waits for them, and re-layouts  6.15 us (10%)
  between operations  0.71 us (1%)
    ppermute x3, waiting for transfers between devices, local(): lax.ppermute(tiles, 'dp', shift(0, k, 0))  9.92 us
    unnamed x20, local copies, waits for them, and re-layouts  6.15 us
    ppermute x3, waiting for transfers between devices, local(): lax.ppermute(part, 'mp', [(i, i ^ k) for i in range(4)])  5.35 us
    ppermute x3, waiting for transfers between devices, local(): lax.ppermute(o, 'mp', [(i, i ^ k) for i in range(4)])  4.56 us
    ppermute x3, starting transfers between devices, local(): lax.ppermute(tiles, 'dp', shift(k, 0, 0))  4.54 us
    pallas_call x1, Pallas kernels, local(): call(project_kernel, [(176, 128)] * 4, [pl.BlockSpec(memory_space=pl.ANY)...  3.99 us
    ppermute x3, waiting for transfers between devices, local(): lax.ppermute(tiles, 'dp', shift(k, 0, 0))  3.98 us
    ppermute x3, starting transfers between devices, local(): lax.ppermute(tiles, 'dp', shift(0, k, 0))  3.84 us
  transfers between devices with their start and end apart: 13, of which 9 were waited for; matrix products, arithmetic and copies ran while one was open for 0% of the time, Pallas kernels for 0%

profile of v1, /device:TPU:1, one launch (start us, length us, event | category | flops | bytes accessed | tf_op | source)
XLA Modules:
  0.0 58.7 jit_solution(17203072297807643872)
XLA Ops:
  0.7 1.5 %copy-done = bf16[4,64,3584]{2,1,0:T(8,128)(2,1)S(1)} copy-done((bf16[4,64,3584]{2,1,0:T(8,128)(2,1)S(1)}, bf16[4,64,3584]{2,1,0:T(8,128)(2,1)}, u32[]{:S(2)}) %copy-start) | copy-done | bytes 1835032
  2.2 1.0 %copy-done.1 = bf16[4,64,1024]{2,1,0:T(8,128)(2,1)S(1)} copy-done((bf16[4,64,1024]{2,1,0:T(8,128)(2,1)S(1)}, bf16[4,64,1024]{2,1,0:T(8,128)(2,1)}, u32[]{:S(2)}) %copy-start.1) | copy-done | bytes 524312
  3.2 1.0 %copy-done.2 = bf16[64,3584]{1,0:T(8,128)(2,1)S(1)} copy-done((bf16[64,3584]{1,0:T(8,128)(2,1)S(1)}, bf16[64,3584]{1,0:T(8,128)(2,1)}, u32[]{:S(2)}) %copy-start.2) | copy-done | bytes 458776
  4.2 0.9 %copy-done.3 = bf16[64,1024]{1,0:T(8,128)(2,1)S(1)} copy-done((bf16[64,1024]{1,0:T(8,128)(2,1)S(1)}, bf16[64,1024]{1,0:T(8,128)(2,1)}, u32[]{:S(2)}) %copy-start.3) | copy-done | bytes 131096
  5.1 0.9 %copy-done.4 = bf16[2,8,3584]{2,1,0:T(8,128)(2,1)S(1)} copy-done((bf16[2,8,3584]{2,1,0:T(8,128)(2,1)S(1)}, bf16[2,8,3584]{2,1,0:T(8,128)(2,1)}, u32[]{:S(2)}) %copy-start.4) | copy-done | bytes 114712
  6.0 0.8 %copy-done.5 = bf16[2,8,1024]{2,1,0:T(8,128)(2,1)S(1)} copy-done((bf16[2,8,1024]{2,1,0:T(8,128)(2,1)S(1)}, bf16[2,8,1024]{2,1,0:T(8,128)(2,1)}, u32[]{:S(2)}) %copy-start.5) | copy-done | bytes 32792
  6.8 4.0 %project.1 = (f32[176,128]{1,0:T(8,128)S(1)}, f32[176,128]{1,0:T(8,128)S(1)}, f32[176,128]{1,0:T(8,128)S(1)}, f32[176,128]{1,0:T(8,128)S(1)}) custom-call(bf16[4,64,1024]{2,1,0:T(8,128)(2,1)S(1)} %copy-done.1, bf16[4,64,3584]{2,1,0:T(8,128)(2,1)S(1)} %copy-done, bf16[16,1024]{1,0:T(8,128)(2,1)S(1)} %bitcast.3, bf16[16,3584]{1,0:T(8,128)(2,1)S(1)} %bitcast.2, ...), custom_call_target="tpu_custom_call" | custom-call | tf_op jit(solution)/shard_map/project/pallas_call | solution.py:210
  10.8 1.5 %collective-permute-start = (f32[176,128]{1,0:T(8,128)S(1)}, f32[176,128]{1,0:T(8,128)S(1)}, u32[]{:S(2)}, u32[]{:S(2)}) collective-permute-start(f32[176,128]{1,0:T(8,128)S(1)} %get-tuple-element.9), channel_id=1, source_target_pairs={{0,1},{1,0},{2,3},{3,2},{4,5},{5,4},{6,7},{7,6},{8,9},{9,8},{10,11... | collective-permute-start | bytes 270344 | tf_op jit(solution)/shard_map/ppermute | solution.py:228
  12.3 1.3 %collective-permute-start.1 = (f32[176,128]{1,0:T(8,128)S(1)}, f32[176,128]{1,0:T(8,128)S(1)}, u32[]{:S(2)}, u32[]{:S(2)}) collective-permute-start(f32[176,128]{1,0:T(8,128)S(1)} %get-tuple-element.10), channel_id=1, source_target_pairs={{0,2},{1,3},{2,0},{3,1},{4,6},{5,7},{6,4},{7,5},{8,10},{9,11},{10,... | collective-permute-start | bytes 270344 | tf_op jit(solution)/shard_map/ppermute | solution.py:228
  13.6 0.4 collective-permute-start.2
  14.0 0.0 collective-permute-done.p1
  14.0 2.4 %collective-permute-done.1.p2 = f32[176,128]{1,0:T(8,128)S(1)} collective-permute-done((f32[176,128]{1,0:T(8,128)S(1)}, f32[176,128]{1,0:T(8,128)S(1)}, u32[]{:S(2)}, u32[]{:S(2)}) %collective-permute-start.1) | collective-permute-done | bytes 90144 | tf_op jit(solution)/shard_map/ppermute | solution.py:228
  16.5 2.1 %collective-permute-done.2.p3 = f32[176,128]{1,0:T(8,128)S(1)} collective-permute-done((f32[176,128]{1,0:T(8,128)S(1)}, f32[176,128]{1,0:T(8,128)S(1)}, u32[]{:S(2)}, u32[]{:S(2)}) %collective-permute-start.2) | collective-permute-done | bytes 90144 | tf_op jit(solution)/shard_map/ppermute | solution.py:228
  18.6 1.0 %features.1 = f32[48,128]{1,0:T(8,128)S(1)} custom-call(s32[4]{0:T(128)S(1)} %copy-done.6, s32[2]{0:T(128)S(1)} %copy-done.7, f32[176,128]{1,0:T(8,128)S(1)} %get-tuple-element.8.p0, f32[176,128]{1,0:T(8,128)S(1)} %collective-permute-done.p1, f32[176,128]{1,0:T(8,128)S(1)} %collective-permute-done.1.p2, f32[176,128]{1,0:T(8,128)S(1)} %collective-permute-done.2.p3), custom_call_target="tpu_custom_call" | custom-call | tf_op jit(solution)/shard_map/features/pallas_call | solution.py:231
  19.5 2.9 %collective-permute-start.3 = (f32[48,128]{1,0:T(8,128)S(1)}, f32[48,128]{1,0:T(8,128)S(1)}, u32[]{:S(2)}, u32[]{:S(2)}) collective-permute-start(f32[48,128]{1,0:T(8,128)S(1)} %features.1), channel_id=1, source_target_pairs={{0,4},{4,0},{8,12},{12,8},{16,20},{20,16},{24,28},{28,24},{32,36},... | collective-permute-start | bytes 73736 | tf_op jit(solution)/shard_map/ppermute | solution.py:238
  22.4 1.4 %collective-permute-done.3 = f32[48,128]{1,0:T(8,128)S(1)} collective-permute-done((f32[48,128]{1,0:T(8,128)S(1)}, f32[48,128]{1,0:T(8,128)S(1)}, u32[]{:S(2)}, u32[]{:S(2)}) %collective-permute-start.3) | collective-permute-done | bytes 24608 | tf_op jit(solution)/shard_map/ppermute | solution.py:238
  23.8 3.8 %collective-permute-start.6 = (f32[96,128]{1,0:T(8,128)S(1)}, f32[96,128]{1,0:T(8,128)S(1)}, u32[]{:S(2)}, u32[]{:S(2)}) collective-permute-start(f32[96,128]{1,0:T(8,128)S(1)} %pad_maximum_fusion), channel_id=1, source_target_pairs={{0,96},{4,100},{8,104},{12,108},{16,112},{20,116},{24,120},{28,124... | collective-permute-start | bytes 147464 | tf_op jit(solution)/shard_map/ppermute | solution.py:240
  27.6 0.7 %collective-permute-start.4 = (f32[96,128]{1,0:T(8,128)S(1)}, f32[96,128]{1,0:T(8,128)S(1)}, u32[]{:S(2)}, u32[]{:S(2)}) collective-permute-start(f32[96,128]{1,0:T(8,128)S(1)} %pad_maximum_fusion), channel_id=1, source_target_pairs={{0,32},{4,36},{8,40},{12,44},{16,48},{20,52},{24,56},{28,60},{32,6... | collective-permute-start | bytes 147464 | tf_op jit(solution)/shard_map/ppermute | solution.py:240
  28.4 4.0 %collective-permute-done.4 = f32[96,128]{1,0:T(8,128)S(1)} collective-permute-done((f32[96,128]{1,0:T(8,128)S(1)}, f32[96,128]{1,0:T(8,128)S(1)}, u32[]{:S(2)}, u32[]{:S(2)}) %collective-permute-start.4) | collective-permute-done | bytes 49184 | tf_op jit(solution)/shard_map/ppermute | solution.py:240
  32.4 2.8 %collective-permute-start.9 = (f32[384,128]{1,0:T(8,128)S(1)}, f32[384,128]{1,0:T(8,128)S(1)}, u32[]{:S(2)}, u32[]{:S(2)}) collective-permute-start(f32[384,128]{1,0:T(8,128)S(1)} %constant_dynamic-update-slice_fusion.y0), channel_id=1, source_target_pairs={{0,24},{4,28},{8,0},{12,4},{16,8},{20,12},{24,16},{28,20},{32,56},... | collective-permute-start | bytes 589832 | tf_op jit(solution)/shard_map/ppermute | solution.py:242
  35.2 0.3 collective-permute-start.8
  35.5 0.7 %collective-permute-start.7 = (f32[384,128]{1,0:T(8,128)S(1)}, f32[384,128]{1,0:T(8,128)S(1)}, u32[]{:S(2)}, u32[]{:S(2)}) collective-permute-start(f32[384,128]{1,0:T(8,128)S(1)} %constant_dynamic-update-slice_fusion.y0), channel_id=1, source_target_pairs={{0,8},{4,12},{8,16},{12,20},{16,24},{20,28},{24,0},{28,4},{32,40},... | collective-permute-start | bytes 589832 | tf_op jit(solution)/shard_map/ppermute | solution.py:242
  36.2 4.0 %collective-permute-done.9.y3 = f32[384,128]{1,0:T(8,128)S(1)} collective-permute-done((f32[384,128]{1,0:T(8,128)S(1)}, f32[384,128]{1,0:T(8,128)S(1)}, u32[]{:S(2)}, u32[]{:S(2)}) %collective-permute-start.9) | collective-permute-done | bytes 196640 | tf_op jit(solution)/shard_map/ppermute | solution.py:242
  40.3 1.1 %collective-permute-done.8.y2 = f32[384,128]{1,0:T(8,128)S(1)} collective-permute-done((f32[384,128]{1,0:T(8,128)S(1)}, f32[384,128]{1,0:T(8,128)S(1)}, u32[]{:S(2)}, u32[]{:S(2)}) %collective-permute-start.8) | collective-permute-done | bytes 196640 | tf_op jit(solution)/shard_map/ppermute | solution.py:242
  41.3 4.8 %collective-permute-done.7.y1 = f32[384,128]{1,0:T(8,128)S(1)} collective-permute-done((f32[384,128]{1,0:T(8,128)S(1)}, f32[384,128]{1,0:T(8,128)S(1)}, u32[]{:S(2)}, u32[]{:S(2)}) %collective-permute-start.7) | collective-permute-done | bytes 196640 | tf_op jit(solution)/shard_map/ppermute | solution.py:242
  46.1 1.3 %gram.1 = (f32[200,128]{1,0:T(8,128)S(1)}, f32[8,192,128]{2,1,0:T(8,128)S(1)}) custom-call(f32[384,128]{1,0:T(8,128)S(1)} %constant_dynamic-update-slice_fusion.y0, f32[384,128]{1,0:T(8,128)S(1)} %collective-permute-done.7.y1, f32[384,128]{1,0:T(8,128)S(1)} %collective-permute-done.8.y2, f32[384,128]{1,0:T(8,128)S(1)} %collective-permute-done.9.y3), custom_call_target="tpu_custom_call" | custom-call | tf_op jit(solution)/shard_map/gram/pallas_call | solution.py:243
  47.5 3.2 %collective-permute-start.12 = (f32[200,128]{1,0:T(8,128)S(1)}, f32[200,128]{1,0:T(8,128)S(1)}, u32[]{:S(2)}, u32[]{:S(2)}) collective-permute-start(f32[200,128]{1,0:T(8,128)S(1)} %get-tuple-element.12.p0), channel_id=1, source_target_pairs={{0,3},{1,2},{2,1},{3,0},{4,7},{5,6},{6,5},{7,4},{8,11},{9,10},{10,... | collective-permute-start | bytes 307208 | tf_op jit(solution)/shard_map/ppermute | solution.py:250
  50.7 0.3 collective-permute-start.11
  50.9 0.2 collective-permute-start.10
  51.1 3.2 %collective-permute-done.12.p3 = f32[200,128]{1,0:T(8,128)S(1)} collective-permute-done((f32[200,128]{1,0:T(8,128)S(1)}, f32[200,128]{1,0:T(8,128)S(1)}, u32[]{:S(2)}, u32[]{:S(2)}) %collective-permute-start.12) | collective-permute-done | bytes 102432 | tf_op jit(solution)/shard_map/ppermute | solution.py:250
  54.3 2.2 %collective-permute-done.11.p2 = f32[200,128]{1,0:T(8,128)S(1)} collective-permute-done((f32[200,128]{1,0:T(8,128)S(1)}, f32[200,128]{1,0:T(8,128)S(1)}, u32[]{:S(2)}, u32[]{:S(2)}) %collective-permute-start.11) | collective-permute-done | bytes 102432 | tf_op jit(solution)/shard_map/ppermute | solution.py:250
  56.5 2.2 %solve.1 = (f32[64,1024]{1,0:T(8,128)}, f32[4,16]{1,0:T(4,128)}) custom-call(f32[200,128]{1,0:T(8,128)S(1)} %get-tuple-element.12.p0, f32[200,128]{1,0:T(8,128)S(1)} %collective-permute-done.10.p1, f32[200,128]{1,0:T(8,128)S(1)} %collective-permute-done.11.p2, f32[200,128]{1,0:T(8,128)S(1)} %collective-permute-done.12.p3, ...), custom_call_target="tpu_custom_call" | custom-call | tf_op jit(solution)/shard_map/solve/pallas_call | solution.py:251
  (20 shorter events, 0.1 us)
Async XLA Ops:
  0.6 18.0 %copy-start.7 = (s32[2]{0:T(128)S(1)}, s32[2]{0:T(128)}, u32[]{:S(2)}) copy-start(s32[2]{0:T(128)} %ql.1) | copy-start | bytes 28
  0.6 17.9 %copy-start.6 = (s32[4]{0:T(128)S(1)}, s32[4]{0:T(128)}, u32[]{:S(2)}) copy-start(s32[4]{0:T(128)} %tl.1) | copy-start | bytes 52
  0.7 1.5 %copy-start = (bf16[4,64,3584]{2,1,0:T(8,128)(2,1)S(1)}, bf16[4,64,3584]{2,1,0:T(8,128)(2,1)}, u32[]{:S(2)}) copy-start(bf16[4,64,3584]{2,1,0:T(8,128)(2,1)} %tg.1) | copy-start | bytes 5505028
  2.2 1.0 %copy-start.1 = (bf16[4,64,1024]{2,1,0:T(8,128)(2,1)S(1)}, bf16[4,64,1024]{2,1,0:T(8,128)(2,1)}, u32[]{:S(2)}) copy-start(bf16[4,64,1024]{2,1,0:T(8,128)(2,1)} %ta.1) | copy-start | bytes 1572868
  3.2 1.0 %copy-start.2 = (bf16[64,3584]{1,0:T(8,128)(2,1)S(1)}, bf16[64,3584]{1,0:T(8,128)(2,1)}, u32[]{:S(2)}) copy-start(bf16[64,3584]{1,0:T(8,128)(2,1)} %po.1) | copy-start | bytes 1376260
  4.2 0.9 %copy-start.3 = (bf16[64,1024]{1,0:T(8,128)(2,1)S(1)}, bf16[64,1024]{1,0:T(8,128)(2,1)}, u32[]{:S(2)}) copy-start(bf16[64,1024]{1,0:T(8,128)(2,1)} %pi.1) | copy-start | bytes 393220
  5.1 0.9 %copy-start.4 = (bf16[2,8,3584]{2,1,0:T(8,128)(2,1)S(1)}, bf16[2,8,3584]{2,1,0:T(8,128)(2,1)}, u32[]{:S(2)}) copy-start(bf16[2,8,3584]{2,1,0:T(8,128)(2,1)} %param.12) | copy-start | bytes 344068
  6.0 0.8 %copy-start.5 = (bf16[2,8,1024]{2,1,0:T(8,128)(2,1)S(1)}, bf16[2,8,1024]{2,1,0:T(8,128)(2,1)}, u32[]{:S(2)}) copy-start(bf16[2,8,1024]{2,1,0:T(8,128)(2,1)} %param.11) | copy-start | bytes 98308
  10.8 3.2 %collective-permute-start = (f32[176,128]{1,0:T(8,128)S(1)}, f32[176,128]{1,0:T(8,128)S(1)}, u32[]{:S(2)}, u32[]{:S(2)}) collective-permute-start(f32[176,128]{1,0:T(8,128)S(1)} %get-tuple-element.9), channel_id=1, source_target_pairs={{0,1},{1,0},{2,3},{3,2},{4,5},{5,4},{6,7},{7,6},{8,9},{9,8},{10,11... | collective-permute-start | bytes 270344 | tf_op jit(solution)/shard_map/ppermute | solution.py:228
  12.3 4.2 %collective-permute-start.1 = (f32[176,128]{1,0:T(8,128)S(1)}, f32[176,128]{1,0:T(8,128)S(1)}, u32[]{:S(2)}, u32[]{:S(2)}) collective-permute-start(f32[176,128]{1,0:T(8,128)S(1)} %get-tuple-element.10), channel_id=1, source_target_pairs={{0,2},{1,3},{2,0},{3,1},{4,6},{5,7},{6,4},{7,5},{8,10},{9,11},{10,... | collective-permute-start | bytes 270344 | tf_op jit(solution)/shard_map/ppermute | solution.py:228
  13.6 5.0 %collective-permute-start.2 = (f32[176,128]{1,0:T(8,128)S(1)}, f32[176,128]{1,0:T(8,128)S(1)}, u32[]{:S(2)}, u32[]{:S(2)}) collective-permute-start(f32[176,128]{1,0:T(8,128)S(1)} %get-tuple-element.11), channel_id=1, source_target_pairs={{0,3},{1,2},{2,1},{3,0},{4,7},{5,6},{6,5},{7,4},{8,11},{9,10},{10,... | collective-permute-start | bytes 270344 | tf_op jit(solution)/shard_map/ppermute | solution.py:228
  19.5 4.3 %collective-permute-start.3 = (f32[48,128]{1,0:T(8,128)S(1)}, f32[48,128]{1,0:T(8,128)S(1)}, u32[]{:S(2)}, u32[]{:S(2)}) collective-permute-start(f32[48,128]{1,0:T(8,128)S(1)} %features.1), channel_id=1, source_target_pairs={{0,4},{4,0},{8,12},{12,8},{16,20},{20,16},{24,28},{28,24},{32,36},... | collective-permute-start | bytes 73736 | tf_op jit(solution)/shard_map/ppermute | solution.py:238
  23.8 8.5 %collective-permute-start.6 = (f32[96,128]{1,0:T(8,128)S(1)}, f32[96,128]{1,0:T(8,128)S(1)}, u32[]{:S(2)}, u32[]{:S(2)}) collective-permute-start(f32[96,128]{1,0:T(8,128)S(1)} %pad_maximum_fusion), channel_id=1, source_target_pairs={{0,96},{4,100},{8,104},{12,108},{16,112},{20,116},{24,120},{28,124... | collective-permute-start | bytes 147464 | tf_op jit(solution)/shard_map/ppermute | solution.py:240
  27.6 4.7 %collective-permute-start.5 = (f32[96,128]{1,0:T(8,128)S(1)}, f32[96,128]{1,0:T(8,128)S(1)}, u32[]{:S(2)}, u32[]{:S(2)}) collective-permute-start(f32[96,128]{1,0:T(8,128)S(1)} %pad_maximum_fusion), channel_id=1, source_target_pairs={{0,64},{4,68},{8,72},{12,76},{16,80},{20,84},{24,88},{28,92},{32,9... | collective-permute-start | bytes 147464 | tf_op jit(solution)/shard_map/ppermute | solution.py:240
  27.6 4.7 %collective-permute-start.4 = (f32[96,128]{1,0:T(8,128)S(1)}, f32[96,128]{1,0:T(8,128)S(1)}, u32[]{:S(2)}, u32[]{:S(2)}) collective-permute-start(f32[96,128]{1,0:T(8,128)S(1)} %pad_maximum_fusion), channel_id=1, source_target_pairs={{0,32},{4,36},{8,40},{12,44},{16,48},{20,52},{24,56},{28,60},{32,6... | collective-permute-start | bytes 147464 | tf_op jit(solution)/shard_map/ppermute | solution.py:240
  32.4 7.9 %collective-permute-start.9 = (f32[384,128]{1,0:T(8,128)S(1)}, f32[384,128]{1,0:T(8,128)S(1)}, u32[]{:S(2)}, u32[]{:S(2)}) collective-permute-start(f32[384,128]{1,0:T(8,128)S(1)} %constant_dynamic-update-slice_fusion.y0), channel_id=1, source_target_pairs={{0,24},{4,28},{8,0},{12,4},{16,8},{20,12},{24,16},{28,20},{32,56},... | collective-permute-start | bytes 589832 | tf_op jit(solution)/shard_map/ppermute | solution.py:242
  35.2 6.1 %collective-permute-start.8 = (f32[384,128]{1,0:T(8,128)S(1)}, f32[384,128]{1,0:T(8,128)S(1)}, u32[]{:S(2)}, u32[]{:S(2)}) collective-permute-start(f32[384,128]{1,0:T(8,128)S(1)} %constant_dynamic-update-slice_fusion.y0), channel_id=1, source_target_pairs={{0,16},{4,20},{8,24},{12,28},{16,0},{20,4},{24,8},{28,12},{32,48},... | collective-permute-start | bytes 589832 | tf_op jit(solution)/shard_map/ppermute | solution.py:242
  35.5 10.6 %collective-permute-start.7 = (f32[384,128]{1,0:T(8,128)S(1)}, f32[384,128]{1,0:T(8,128)S(1)}, u32[]{:S(2)}, u32[]{:S(2)}) collective-permute-start(f32[384,128]{1,0:T(8,128)S(1)} %constant_dynamic-update-slice_fusion.y0), channel_id=1, source_target_pairs={{0,8},{4,12},{8,16},{12,20},{16,24},{20,28},{24,0},{28,4},{32,40},... | collective-permute-start | bytes 589832 | tf_op jit(solution)/shard_map/ppermute | solution.py:242
  47.5 6.8 %collective-permute-start.12 = (f32[200,128]{1,0:T(8,128)S(1)}, f32[200,128]{1,0:T(8,128)S(1)}, u32[]{:S(2)}, u32[]{:S(2)}) collective-permute-start(f32[200,128]{1,0:T(8,128)S(1)} %get-tuple-element.12.p0), channel_id=1, source_target_pairs={{0,3},{1,2},{2,1},{3,0},{4,7},{5,6},{6,5},{7,4},{8,11},{9,10},{10,... | collective-permute-start | bytes 307208 | tf_op jit(solution)/shard_map/ppermute | solution.py:250
  50.7 5.8 %collective-permute-start.11 = (f32[200,128]{1,0:T(8,128)S(1)}, f32[200,128]{1,0:T(8,128)S(1)}, u32[]{:S(2)}, u32[]{:S(2)}) collective-permute-start(f32[200,128]{1,0:T(8,128)S(1)} %get-tuple-element.12.p0), channel_id=1, source_target_pairs={{0,2},{1,3},{2,0},{3,1},{4,6},{5,7},{6,4},{7,5},{8,10},{9,11},{10,... | collective-permute-start | bytes 307208 | tf_op jit(solution)/shard_map/ppermute | solution.py:250
  50.9 5.6 %collective-permute-start.10 = (f32[200,128]{1,0:T(8,128)S(1)}, f32[200,128]{1,0:T(8,128)S(1)}, u32[]{:S(2)}, u32[]{:S(2)}) collective-permute-start(f32[200,128]{1,0:T(8,128)S(1)} %get-tuple-element.12.p0), channel_id=1, source_target_pairs={{0,1},{1,0},{2,3},{3,2},{4,5},{5,4},{6,7},{7,6},{8,9},{9,8},{10,11... | collective-permute-start | bytes 307208 | tf_op jit(solution)/shard_map/ppermute | solution.py:250

commit v2 on v1

--- a/solution.py
+++ b/solution.py
@@ -100,16 +100,14 @@
         feats[32 + 8 * r : 40 + 8 * r, :] = jnp.where(low, even, odd) * (1.0 / math.sqrt(8.0))
 
 
-def gram_kernel(y0, y1, y2, y3, part, fq, fs, qs):
-    dp = lax.axis_index("dp")
-    mz, my, mx = dp // (NY * NX), (dp // NX) % NY, dp % NX
-    for j, ref in enumerate((y0, y1, y2, y3)):
-        for k in range(NZ):
-            for e in range(NX):
-                slot = ((mz + NZ - k) % NZ * NY + (my + NY - j) % NY) * NX + (mx ^ e)
-                at = 48 * (2 * k + e)
-                fs[pl.ds(pl.multiple_of(slot * 32, 32), 32), :] = ref[at : at + 32, :]
-                qs[pl.ds(pl.multiple_of(slot * 16, 16), 16), :] = ref[at + 32 : at + 48, :]
+def gram_kernel(tiles, part, fq, fs, qs):
+    mx = lax.axis_index("dp") % NX
+    for s in range(NZ * NY):
+        for e in range(NX):
+            slot = NX * s + e
+            at = 48 * (NX * s + e)
+            fs[pl.ds(pl.multiple_of(slot * 32, 32), 32), :] = tiles[at : at + 32, :]
+            qs[pl.ds(pl.multiple_of(slot * 16, 16), 16), :] = tiles[at + 32 : at + 48, :]
     total = jnp.zeros((192, 128), jnp.float32)
     squares = jnp.zeros((64, 128), jnp.float32)
     for a in range(8):
@@ -119,20 +117,35 @@
         fq[a, 128:192, :] = q
         total += dot(jnp.concatenate([f, q], axis=0), f, NT)
         squares += q * q
-    part[0:192, :] = total
-    norms = dot(jnp.ones((8, 128), jnp.float32), squares, NT)
-    part[192:200, :] = jnp.concatenate([norms, norms], axis=1)
+    ones = jnp.ones((8, 128), jnp.float32)
+    row = lax.broadcasted_iota(jnp.int32, (64, 64), 0)
+    col = lax.broadcasted_iota(jnp.int32, (64, 64), 1)
+    both = jnp.where(row >= col, total[64:128, 64:128], total[0:64, 0:64])
+    part[0:64, :] = jnp.concatenate([total[64:128, 0:64], both], axis=1)
+    part[64:128, :] = total[128:192]
+    diag = jnp.sum(jnp.where(row == col, total[0:64, 0:64], 0.0), axis=0, keepdims=True)
+    norms = dot(ones, squares, NT)
+    part[128:136, :] = jnp.concatenate([norms, jnp.broadcast_to(diag, (8, 64))], axis=1)
 
 
 def solve_kernel(p0, p1, p2, p3, fq, precond, scores, ys):
     dp = lax.axis_index("dp")
     me = lax.axis_index("mp")
     x = (p0[...] + p1[...]) + (p2[...] + p3[...])
-    gram = x[0:128]
-    cross = x[128:192]
-    row = lax.broadcasted_iota(jnp.int32, (64, 128), 0)
-    col = lax.broadcasted_iota(jnp.int32, (64, 128), 1)
-    norm_q = jnp.sum(jnp.where(row == col, jnp.broadcast_to(x[192:193], (64, 128)), 0.0),
+    row = lax.broadcasted_iota(jnp.int32, (64, 64), 0)
+    col = lax.broadcasted_iota(jnp.int32, (64, 64), 1)
+    both = x[0:64, 64:128]
+    flip = both.T
+    diag = jnp.broadcast_to(x[128:129, 64:128], (64, 64))
+    upper = jnp.where(row < col, both, jnp.where(row > col, flip, diag))
+    lower = jnp.where(row < col, flip, both)
+    corner = x[0:64, 0:64]
+    gram = jnp.concatenate(
+        [jnp.concatenate([upper, corner.T], axis=1), jnp.concatenate([corner, lower], axis=1)],
+        axis=0,
+    )
+    cross = x[64:128]
+    norm_q = jnp.sum(jnp.where(row == col, jnp.broadcast_to(x[128:129, 0:64], (64, 64)), 0.0),
                      axis=1, keepdims=True)
     grow = lax.broadcasted_iota(jnp.int32, (128, 128), 0)
     gcol = lax.broadcasted_iota(jnp.int32, (128, 128), 1)
@@ -190,19 +203,6 @@
     )
 
 
-def dp_index(z, y, x):
-    return (z * NY + y) * NX + x
-
-
-def shift(dz, dy, dx):
-    return [
-        (dp_index(z, y, x), dp_index((z + dz) % NZ, (y + dy) % NY, (x + dx) % NX))
-        for z in range(NZ)
-        for y in range(NY)
-        for x in range(NX)
-    ]
-
-
 def local(train_acts, train_grads, train_lengths, query_acts, query_grads, query_lengths,
           proj_in, proj_out):
     d, ff = proj_in.shape[1], proj_out.shape[1]
@@ -210,7 +210,7 @@
     own, *others = call(
         project_kernel,
         [(176, 128)] * 4,
-        [pl.BlockSpec(memory_space=pl.ANY)] * 6,
+        [pl.BlockSpec(memory_space=pltpu.HBM)] * 6,
         [
             pltpu.VMEM((4, 64, d), bf),
             pltpu.VMEM((4, 64, ff), bf),
@@ -222,11 +222,15 @@
             pltpu.SemaphoreType.DMA((9,)),
         ],
         "project",
-    )(train_acts, train_grads, query_acts.reshape(16, d), query_grads.reshape(16, ff),
-      proj_in, proj_out)
+    )(*(pltpu.with_memory_space_constraint(a, pltpu.HBM)
+        for a in (train_acts, train_grads, query_acts.reshape(16, d),
+                  query_grads.reshape(16, ff), proj_in, proj_out)))
     got = [
         lax.ppermute(o, "mp", [(i, i ^ k) for i in range(4)]) for k, o in zip((1, 2, 3), others)
     ]
+    dp = NZ * NY * NX
+    swap_x = [(i, i ^ 1) for i in range(dp)]
+    planes = [list(range(x, dp, NX)) for x in range(NX)]
     smem = pl.BlockSpec(memory_space=pltpu.SMEM)
     (tiles,) = call(
         features_kernel,
@@ -235,18 +239,15 @@
         [pltpu.VMEM((64, 128), jnp.float32), pltpu.VMEM((128, 128), jnp.float32)],
         "features",
     )(train_lengths, query_lengths, own, *got)
-    tiles = jnp.concatenate([tiles, lax.ppermute(tiles, "dp", shift(0, 0, 1))], axis=0)
-    tiles = jnp.concatenate(
-        [tiles] + [lax.ppermute(tiles, "dp", shift(k, 0, 0)) for k in range(1, NZ)], axis=0
-    )
-    planes = [tiles] + [lax.ppermute(tiles, "dp", shift(0, k, 0)) for k in range(1, NY)]
+    tiles = jnp.broadcast_to(tiles[None], (dp, 48, 128))
+    tiles = lax.all_to_all(tiles, "dp", 0, 0, tiled=True)
     part, fq = call(
         gram_kernel,
-        [(200, 128), (8, 192, 128)],
-        whole(4),
+        [(136, 128), (8, 192, 128)],
+        whole(1),
         [pltpu.VMEM((1024, 128), jnp.float32), pltpu.VMEM((512, 128), jnp.float32)],
         "gram",
-    )(*planes)
+    )(tiles.reshape(-1, 128))
     got = [lax.ppermute(part, "mp", [(i, i ^ k) for i in range(4)]) for k in (1, 2, 3)]
     precond, scores = call(
         solve_kernel,

time: 59 us -> 49.5 us (0.84)
  blocking collectives: 0 us -> 26.3 us
  waiting for transfers between devices: 25.2 us -> 7.91 us
  starting transfers between devices: 18.2 us -> 6.29 us
  local copies, waits for them, and re-layouts: 6.15 us -> 0.06 us
    all_to_all x0 -> x1, blocking collectives: none -> 26.3 us  [local(): tiles = lax.all_to_all(tiles, 'dp', 0, 0, tiled=True)]
    ppermute x7 -> x0, waiting for transfers between devices: 15.3 us -> none  [the longest x3 9.92 us: local(): lax.ppermute(tiles, 'dp', shift(0, k, 0))]
    ppermute x7 -> x0, starting transfers between devices: 11.3 us -> none  [the longest x3 4.54 us: local(): lax.ppermute(tiles, 'dp', shift(k, 0, 0))]
    unnamed x20 -> x4, local copies, waits for them, and re-layouts: 6.15 us -> 0.01 us
    ppermute x3, waiting for transfers between devices: 5.35 us -> 3.35 us  [local(): lax.ppermute(part, 'mp', [(i, i ^ k) for i in range(4)])]
    ppermute x3, starting transfers between devices: 3.68 us -> 3.07 us  [local(): lax.ppermute(part, 'mp', [(i, i ^ k) for i in range(4)])]
  transfers between devices with their start and end apart: 13 -> 6, of which waited for: 9 -> 4; matrix products, arithmetic and copies ran while one was open for 0% -> 0% of each run, Pallas kernels for 0% -> 0%
where the time goes in v2:
time: 49.5 us; the launch traced here: 49.3 us
  blocking collectives  26.3 us (53%)
  Pallas kernels  8.14 us (16%)
  waiting for transfers between devices  7.91 us (16%)
  starting transfers between devices  6.29 us (13%)
  between operations  0.67 us (1%)
    all_to_all x1, blocking collectives, local(): tiles = lax.all_to_all(tiles, 'dp', 0, 0, tiled=True)  26.3 us
    ppermute x3, waiting for transfers between devices, local(): lax.ppermute(o, 'mp', [(i, i ^ k) for i in range(4)])  4.56 us
    pallas_call x1, Pallas kernels, local(): call(project_kernel, [(176, 128)] * 4, [pl.BlockSpec(memory_space=pltpu.H...  3.4 us
    ppermute x3, waiting for transfers between devices, local(): lax.ppermute(part, 'mp', [(i, i ^ k) for i in range(4)])  3.35 us
    ppermute x3, starting transfers between devices, local(): lax.ppermute(o, 'mp', [(i, i ^ k) for i in range(4)])  3.22 us
    ppermute x3, starting transfers between devices, local(): lax.ppermute(part, 'mp', [(i, i ^ k) for i in range(4)])  3.07 us
    pallas_call x1, Pallas kernels, local(): call(solve_kernel, [(64, 1024), (4, 16)], whole(5), [pltpu.VMEM((64, 128)...  2.44 us
    pallas_call x1, Pallas kernels, local(): call(gram_kernel, [(136, 128), (8, 192, 128)], whole(1), [pltpu.VMEM((102...  1.34 us
  transfers between devices with their start and end apart: 6, of which 4 were waited for; matrix products, arithmetic and copies ran while one was open for 0% of the time, Pallas kernels for 0%

profile of v2, /device:TPU:1, one launch (start us, length us, event | category | flops | bytes accessed | tf_op | source)
XLA Modules:
  0.0 49.3 jit_solution(2492265263860011413)
XLA Ops:
  0.6 0.0 copy-start.1
  0.6 0.0 copy-start
  0.7 3.4 %project.1 = (f32[176,128]{1,0:T(8,128)S(1)}, f32[176,128]{1,0:T(8,128)S(1)}, f32[176,128]{1,0:T(8,128)S(1)}, f32[176,128]{1,0:T(8,128)S(1)}) custom-call(bf16[4,64,1024]{2,1,0:T(8,128)(2,1)} %ta.1, bf16[4,64,3584]{2,1,0:T(8,128)(2,1)} %tg.1, bf16[16,1024]{1,0:T(8,128)(2,1)} %bitcast.5, bf16[16,3584]{1,0:T(8,128)(2,1)} %bitcast.4, bf16[64,1024]{1,0:T(8,128)(2,1)} %pi.1, ...), custom_call_target="tpu_custom_call" | custom-call | tf_op jit(solution)/shard_map/project/pallas_call | solution.py:210
  4.1 1.5 %collective-permute-start = (f32[176,128]{1,0:T(8,128)S(1)}, f32[176,128]{1,0:T(8,128)S(1)}, u32[]{:S(2)}, u32[]{:S(2)}) collective-permute-start(f32[176,128]{1,0:T(8,128)S(1)} %get-tuple-element.9), channel_id=1, source_target_pairs={{0,1},{1,0},{2,3},{3,2},{4,5},{5,4},{6,7},{7,6},{8,9},{9,8},{10,11... | collective-permute-start | bytes 270344 | tf_op jit(solution)/shard_map/ppermute | solution.py:229
  5.6 1.3 %collective-permute-start.1 = (f32[176,128]{1,0:T(8,128)S(1)}, f32[176,128]{1,0:T(8,128)S(1)}, u32[]{:S(2)}, u32[]{:S(2)}) collective-permute-start(f32[176,128]{1,0:T(8,128)S(1)} %get-tuple-element.10), channel_id=1, source_target_pairs={{0,2},{1,3},{2,0},{3,1},{4,6},{5,7},{6,4},{7,5},{8,10},{9,11},{10,... | collective-permute-start | bytes 270344 | tf_op jit(solution)/shard_map/ppermute | solution.py:229
  6.9 0.4 collective-permute-start.2
  7.3 0.0 collective-permute-done.p1
  7.3 2.4 %collective-permute-done.1.p2 = f32[176,128]{1,0:T(8,128)S(1)} collective-permute-done((f32[176,128]{1,0:T(8,128)S(1)}, f32[176,128]{1,0:T(8,128)S(1)}, u32[]{:S(2)}, u32[]{:S(2)}) %collective-permute-start.1) | collective-permute-done | bytes 90144 | tf_op jit(solution)/shard_map/ppermute | solution.py:229
  9.7 2.1 %collective-permute-done.2.p3 = f32[176,128]{1,0:T(8,128)S(1)} collective-permute-done((f32[176,128]{1,0:T(8,128)S(1)}, f32[176,128]{1,0:T(8,128)S(1)}, u32[]{:S(2)}, u32[]{:S(2)}) %collective-permute-start.2) | collective-permute-done | bytes 90144 | tf_op jit(solution)/shard_map/ppermute | solution.py:229
  11.8 0.0 copy-done.1
  11.8 0.0 copy-done
  11.9 1.0 %features.1 = f32[48,128]{1,0:T(8,128)S(1)} custom-call(s32[4]{0:T(128)S(1)} %copy-done, s32[2]{0:T(128)S(1)} %copy-done.1, f32[176,128]{1,0:T(8,128)S(1)} %get-tuple-element.8.p0, f32[176,128]{1,0:T(8,128)S(1)} %collective-permute-done.p1, f32[176,128]{1,0:T(8,128)S(1)} %collective-permute-done.1.p2, f32[176,128]{1,0:T(8,128)S(1)} %collective-permute-done.2.p3), custom_call_target="tpu_custom_call" | custom-call | tf_op jit(solution)/shard_map/features/pallas_call | solution.py:235
  12.8 0.1 broadcast_in_dim.2
  12.9 26.3 %all_to_all.5 = f32[32,48,128]{2,1,0:T(8,128)S(1)} all-to-all(f32[32,48,128]{2,1,0:T(8,128)S(1)} %broadcast_in_dim.2), channel_id=1, replica_groups=mesh['dp'=32,'mp'=4] {'dp'}, dimensions={0} | all-to-all | bytes 1572864 | tf_op jit(solution)/shard_map/all_to_all | solution.py:243
  39.1 1.3 %gram.1 = (f32[136,128]{1,0:T(8,128)S(1)}, f32[8,192,128]{2,1,0:T(8,128)S(1)}) custom-call(f32[1536,128]{1,0:T(8,128)S(1)} %bitcast.3), custom_call_target="tpu_custom_call" | custom-call | tf_op jit(solution)/shard_map/gram/pallas_call | solution.py:244
  40.5 1.9 %collective-permute-start.5 = (f32[136,128]{1,0:T(8,128)S(1)}, f32[136,128]{1,0:T(8,128)S(1)}, u32[]{:S(2)}, u32[]{:S(2)}) collective-permute-start(f32[136,128]{1,0:T(8,128)S(1)} %get-tuple-element.12.p0), channel_id=1, source_target_pairs={{0,3},{1,2},{2,1},{3,0},{4,7},{5,6},{6,5},{7,4},{8,11},{9,10},{10,... | collective-permute-start | bytes 208904 | tf_op jit(solution)/shard_map/ppermute | solution.py:251
  42.4 1.2 %collective-permute-start.4 = (f32[136,128]{1,0:T(8,128)S(1)}, f32[136,128]{1,0:T(8,128)S(1)}, u32[]{:S(2)}, u32[]{:S(2)}) collective-permute-start(f32[136,128]{1,0:T(8,128)S(1)} %get-tuple-element.12.p0), channel_id=1, source_target_pairs={{0,2},{1,3},{2,0},{3,1},{4,6},{5,7},{6,4},{7,5},{8,10},{9,11},{10,... | collective-permute-start | bytes 208904 | tf_op jit(solution)/shard_map/ppermute | solution.py:251
  43.5 0.0 collective-permute-start.3
  43.5 0.8 %collective-permute-done.5.p3 = f32[136,128]{1,0:T(8,128)S(1)} collective-permute-done((f32[136,128]{1,0:T(8,128)S(1)}, f32[136,128]{1,0:T(8,128)S(1)}, u32[]{:S(2)}, u32[]{:S(2)}) %collective-permute-start.5) | collective-permute-done | bytes 69664 | tf_op jit(solution)/shard_map/ppermute | solution.py:251
  44.4 2.5 %collective-permute-done.4.p2 = f32[136,128]{1,0:T(8,128)S(1)} collective-permute-done((f32[136,128]{1,0:T(8,128)S(1)}, f32[136,128]{1,0:T(8,128)S(1)}, u32[]{:S(2)}, u32[]{:S(2)}) %collective-permute-start.4) | collective-permute-done | bytes 69664 | tf_op jit(solution)/shard_map/ppermute | solution.py:251
  46.9 0.0 collective-permute-done.3.p1
  46.9 2.4 %solve.1 = (f32[64,1024]{1,0:T(8,128)}, f32[4,16]{1,0:T(4,128)}) custom-call(f32[136,128]{1,0:T(8,128)S(1)} %get-tuple-element.12.p0, f32[136,128]{1,0:T(8,128)S(1)} %collective-permute-done.3.p1, f32[136,128]{1,0:T(8,128)S(1)} %collective-permute-done.4.p2, f32[136,128]{1,0:T(8,128)S(1)} %collective-permute-done.5.p3, f32[8,192,128]{2,1,0:T(8,128)S(1)} %get-tuple-element.13.fq), custom_call_target="tpu_custom_call" | custom-call | tf_op jit(solution)/shard_map/solve/pallas_call | solution.py:252
Async XLA Ops:
  0.6 11.2 %copy-start.1 = (s32[2]{0:T(128)S(1)}, s32[2]{0:T(128)}, u32[]{:S(2)}) copy-start(s32[2]{0:T(128)} %ql.1) | copy-start | bytes 28
  0.6 11.2 %copy-start = (s32[4]{0:T(128)S(1)}, s32[4]{0:T(128)}, u32[]{:S(2)}) copy-start(s32[4]{0:T(128)} %tl.1) | copy-start | bytes 52
  4.1 3.2 %collective-permute-start = (f32[176,128]{1,0:T(8,128)S(1)}, f32[176,128]{1,0:T(8,128)S(1)}, u32[]{:S(2)}, u32[]{:S(2)}) collective-permute-start(f32[176,128]{1,0:T(8,128)S(1)} %get-tuple-element.9), channel_id=1, source_target_pairs={{0,1},{1,0},{2,3},{3,2},{4,5},{5,4},{6,7},{7,6},{8,9},{9,8},{10,11... | collective-permute-start | bytes 270344 | tf_op jit(solution)/shard_map/ppermute | solution.py:229
  5.6 4.2 %collective-permute-start.1 = (f32[176,128]{1,0:T(8,128)S(1)}, f32[176,128]{1,0:T(8,128)S(1)}, u32[]{:S(2)}, u32[]{:S(2)}) collective-permute-start(f32[176,128]{1,0:T(8,128)S(1)} %get-tuple-element.10), channel_id=1, source_target_pairs={{0,2},{1,3},{2,0},{3,1},{4,6},{5,7},{6,4},{7,5},{8,10},{9,11},{10,... | collective-permute-start | bytes 270344 | tf_op jit(solution)/shard_map/ppermute | solution.py:229
  6.9 5.0 %collective-permute-start.2 = (f32[176,128]{1,0:T(8,128)S(1)}, f32[176,128]{1,0:T(8,128)S(1)}, u32[]{:S(2)}, u32[]{:S(2)}) collective-permute-start(f32[176,128]{1,0:T(8,128)S(1)} %get-tuple-element.11), channel_id=1, source_target_pairs={{0,3},{1,2},{2,1},{3,0},{4,7},{5,6},{6,5},{7,4},{8,11},{9,10},{10,... | collective-permute-start | bytes 270344 | tf_op jit(solution)/shard_map/ppermute | solution.py:229
  40.5 3.9 %collective-permute-start.5 = (f32[136,128]{1,0:T(8,128)S(1)}, f32[136,128]{1,0:T(8,128)S(1)}, u32[]{:S(2)}, u32[]{:S(2)}) collective-permute-start(f32[136,128]{1,0:T(8,128)S(1)} %get-tuple-element.12.p0), channel_id=1, source_target_pairs={{0,3},{1,2},{2,1},{3,0},{4,7},{5,6},{6,5},{7,4},{8,11},{9,10},{10,... | collective-permute-start | bytes 208904 | tf_op jit(solution)/shard_map/ppermute | solution.py:251
  42.4 4.5 %collective-permute-start.4 = (f32[136,128]{1,0:T(8,128)S(1)}, f32[136,128]{1,0:T(8,128)S(1)}, u32[]{:S(2)}, u32[]{:S(2)}) collective-permute-start(f32[136,128]{1,0:T(8,128)S(1)} %get-tuple-element.12.p0), channel_id=1, source_target_pairs={{0,2},{1,3},{2,0},{3,1},{4,6},{5,7},{6,4},{7,5},{8,10},{9,11},{10,... | collective-permute-start | bytes 208904 | tf_op jit(solution)/shard_map/ppermute | solution.py:251
  43.5 3.4 %collective-permute-start.3 = (f32[136,128]{1,0:T(8,128)S(1)}, f32[136,128]{1,0:T(8,128)S(1)}, u32[]{:S(2)}, u32[]{:S(2)}) collective-permute-start(f32[136,128]{1,0:T(8,128)S(1)} %get-tuple-element.12.p0), channel_id=1, source_target_pairs={{0,1},{1,0},{2,3},{3,2},{4,5},{5,4},{6,7},{7,6},{8,9},{9,8},{10,11... | collective-permute-start | bytes 208904 | tf_op jit(solution)/shard_map/ppermute | solution.py:251

commit v3 on v2

v3 whole, which is shorter than its diff:
```python
import math

import jax
import jax.numpy as jnp
from jax import lax
from jax.experimental import pallas as pl
from jax.experimental.pallas import tpu as pltpu
from jax.sharding import PartitionSpec as P

ITERS = 4
DAMPING = 0.5
EPSILON = 1e-06
ROWS, QUERIES, RANK, LEN, QLEN = 128, 64, 64, 64, 8
VMEM = 48 * 2**20

NT = (((1,), (1,)), ((), ()))
NN = (((1,), (0,)), ((), ()))
TN = (((0,), (0,)), ((), ()))


def mm(a, b, dims):
    return lax.dot_general(a, b, dims, preferred_element_type=jnp.float32)


def split(x):
    high = x.astype(jnp.bfloat16)
    return high, (x - high.astype(jnp.float32)).astype(jnp.bfloat16)


def project_kernel(ta, tg, qa, qg, pi, po, keep, give, a_v, g_v, pi_v, po_v, out_t, sems):
    rows, length, ff = tg.shape
    slots = rows * length
    half = ff // 2
    count = iter(range(32))

    def load(src, dst):
        return pltpu.make_async_copy(src, dst, sems.at[next(count)])

    groups = [[load(pi, pi_v), load(qa, a_v.at[slots : slots + 16])]]
    for r in range(rows):
        groups[0].append(load(ta.at[r], a_v.at[length * r : length * (r + 1)]))
    for c in range(2):
        cols = pl.ds(half * c, half)
        group = [load(po.at[:, cols], po_v.at[:, cols]),
                 load(qg.at[:, cols], g_v.at[slots : slots + 16, cols])]
        for r in range(rows):
            group.append(load(tg.at[r, :, cols], g_v.at[length * r : length * (r + 1), cols]))
        groups.append(group)
    for group in groups:
        for c in group:
            c.start()
    me = lax.axis_index("mp")
    for c in groups[0]:
        c.wait()
    inn = mm(a_v[...], pi_v[...], NT)
    train_in = inn[0:slots].T
    for o in (keep, give):
        o[32:96, :] = train_in[:, 0:128]
        o[96:160, :] = train_in[:, 128:256]
    out = None
    for k in range(2):
        for c in groups[k + 1]:
            c.wait()
        cols = slice(half * k, half * (k + 1))
        term = mm(g_v[:, cols], po_v[:, cols], NT)
        out = term if out is None else out + term
    queries = jnp.concatenate([inn[slots:], out[slots:]], axis=1)
    out_t[...] = out[0:slots].T
    for core, o in enumerate((keep, give)):
        o[160:176, :] = queries
        for chip, at in enumerate((0, 176)):
            who = me ^ (core + 2 * chip)
            quarter = out_t[pl.ds(pl.multiple_of(who * 16, 16), 16), :]
            o[at : at + 16, :] = quarter[:, 0:128]
            o[at + 16 : at + 32, :] = quarter[:, 128:256]


def dot3(a, b, axis):
    ah, al = split(a)
    bh, bl = split(b)
    dims = NT if axis == 1 else TN
    return mm(jnp.concatenate([ah, ah, al], axis=axis), jnp.concatenate([bh, bl, bh], axis=axis), dims)


def features_kernel(tl, ql, mine, got, feats, scr, qscr):
    me = lax.axis_index("mp")
    lane = lax.broadcasted_iota(jnp.int32, (16, 128), 1)
    low = lax.broadcasted_iota(jnp.int32, (8, 128), 1) < 64
    for pair in range(2):
        out = mine[16 * pair : 16 * pair + 16] + got[144 + 16 * pair : 160 + 16 * pair]
        inn = mine[32 + 64 * pair : 96 + 64 * pair] + got[64 * pair : 64 * pair + 64]
        first = jnp.where(lane < jnp.minimum(tl[2 * pair], 64), out, 0.0)
        second = jnp.where((lane >= 64) & (lane < 64 + tl[2 * pair + 1]), out, 0.0)
        left = jnp.concatenate([first, second], axis=0)
        right = jnp.concatenate([inn, inn], axis=0)
        scr[32 * pair : 32 * pair + 32, :] = dot3(left, right, 1)
    for r in range(4):
        even = scr[pl.ds(16 * r, 8, stride=2), :]
        odd = scr[pl.ds(16 * r + 1, 8, stride=2), :]
        feats[8 * r : 8 * r + 8, :] = jnp.where(low, even, odd) * (1.0 / math.sqrt(LEN))
    q = mine[160:176] + got[128:144]
    slot = lax.broadcasted_iota(jnp.int32, (16, 64), 0)
    qin = q[:, 0:64]
    qout = q[:, 64:128]
    first = jnp.where(slot < ql[0], qout, 0.0)
    second = jnp.where((slot >= 8) & (slot < 8 + ql[1]), qout, 0.0)
    qscr[...] = dot3(jnp.concatenate([first, second], axis=1), jnp.concatenate([qin, qin], axis=1), 0)
    for r in range(2):
        scr[16 * r : 16 * r + 16, :] = qscr[pl.ds(pl.multiple_of(64 * r + me * 16, 16), 16), :]
    for r in range(2):
        even = scr[pl.ds(16 * r, 8, stride=2), :]
        odd = scr[pl.ds(16 * r + 1, 8, stride=2), :]
        feats[32 + 8 * r : 40 + 8 * r, :] = jnp.where(low, even, odd) * (1.0 / math.sqrt(QLEN))


def gram_kernel(tiles, part, xh_ref, xl_ref):
    for a in range(8):
        cols = [tiles[pl.ds(8 * r + a, 32, stride=48), :] for r in range(6)]
        high, low = split(jnp.concatenate(cols, axis=0))
        xh_ref[:, 128 * a : 128 * a + 128] = high
        xl_ref[:, 128 * a : 128 * a + 128] = low
    xh, xl = xh_ref[...], xl_ref[...]
    fh = xh[0:128]
    total = mm(xh, xh, NT) + mm(xh, xl, NT) + mm(xl, xh, NT)
    row = lax.broadcasted_iota(jnp.int32, (64, 64), 0)
    col = lax.broadcasted_iota(jnp.int32, (64, 64), 1)

    def diagonal(block):
        return jnp.sum(jnp.where(row == col, block, 0.0), axis=0, keepdims=True)

    first = total[0:64, 0:64]
    both = jnp.where(row >= col, total[64:128, 64:128], first)
    part[0:64, :] = jnp.concatenate([total[64:128, 0:64], both], axis=1)
    part[64:128, :] = jnp.concatenate([total[0:64, 128:192], total[64:128, 128:192]], axis=1)
    tail = jnp.concatenate([diagonal(total[128:192, 128:192]), diagonal(first)], axis=1)
    part[128:136, :] = jnp.broadcast_to(tail, (8, 128))


def solve_kernel(mine, got, xh, xl, precond, scores, ys, ts):
    dp = lax.axis_index("dp")
    me = lax.axis_index("mp")
    x = mine[...] + got[...]
    row = lax.broadcasted_iota(jnp.int32, (64, 64), 0)
    col = lax.broadcasted_iota(jnp.int32, (64, 64), 1)
    corner, both = x[0:64, 0:64], x[0:64, 64:128]
    flip = both.T
    diag = x[128:129, 64:128]
    upper = jnp.where(row < col, both, jnp.where(row > col, flip, diag))
    lower = jnp.where(row < col, flip, both)
    gram = jnp.concatenate(
        [jnp.concatenate([upper, corner.T], axis=1), jnp.concatenate([corner, lower], axis=1)],
        axis=0,
    )
    cross = jnp.concatenate([x[64:128, 0:64], x[64:128, 64:128]], axis=0)
    norm_q = x[128:129, 0:64]
    trace = jnp.sum(diag + jnp.sum(jnp.where(row == col, both, 0.0), axis=0, keepdims=True),
                    axis=1, keepdims=True)
    damp = trace * (DAMPING / (ROWS * RANK * RANK)) + EPSILON
    inv_rows = 1.0 / ROWS
    gh, gl = split(gram)
    stacked = jnp.concatenate([gh, gl], axis=0)

    def times_gram(y):
        yh, yl = split(y)
        t = mm(stacked, jnp.concatenate([yh, yl], axis=1), NN)
        t = t[0:128] + t[128:256]
        return t[:, 0:64] + t[:, 64:128]

    def total(v):
        return jnp.sum(v, axis=0, keepdims=True)

    def inner(alpha, w, y):
        return alpha * alpha * norm_q + total(w * (alpha * cross + y))

    ra, rw, ry = jnp.ones((1, 64), jnp.float32), jnp.zeros((128, 64), jnp.float32), cross
    da, dw, dy = ra, rw, ry
    za, zw, zy = jnp.zeros((1, 64), jnp.float32), rw, rw
    rr = norm_q
    dd = norm_q
    for step in range(ITERS):
        curvature = damp * dd + total(dy * dy) * inv_rows
        size = rr / curvature
        za, zw, zy = za + size * da, zw + size * dw, zy + size * dy
        if step == ITERS - 1:
            break
        iy = damp * dy + times_gram(dy) * inv_rows
        ra = ra - size * (damp * da)
        rw = rw - size * (damp * dw + dy * inv_rows)
        ry = ry - size * iy
        new = inner(ra, rw, ry)
        ratio = new / rr
        da, dw, dy = ra + ratio * da, rw + ratio * dw, ry + ratio * dy
        rr = new
        dd = inner(da, dw, dy)
    weights = jnp.concatenate([zw, jnp.where(row == col, za, 0.0)], axis=0)
    turned = weights.T
    pad = jnp.zeros((32, 64), jnp.float32)
    for k in range(2):
        turn = turned[32 * k : 32 * k + 32]
        ts[pl.ds(k, 32, stride=2), :] = turn[:, 0:128]
        ts[pl.ds(64 + k, 32, stride=2), :] = jnp.concatenate([turn[:, 128:192], pad], axis=1)
    wh, wl = split(jnp.concatenate([ts[0:64, :], ts[64:128, 0:64]], axis=1))
    ys[...] = jnp.concatenate([zy, jnp.zeros_like(zy)], axis=1)
    high = xh[...]
    z = mm(jnp.concatenate([wh, wl], axis=0), high, NN)
    precond[...] = z[0:64] + z[64:128] + mm(wh, xl[...], NN)
    mine_rows = ys[pl.ds(dp, 4, stride=32), :][:, 0:64]
    slot = lax.broadcasted_iota(jnp.int32, (64, 16), 0)
    want = lax.broadcasted_iota(jnp.int32, (64, 16), 1)
    pick = (slot == (want % 2) * 32 + 8 * me + want // 2).astype(jnp.float32)
    scores[...] = lax.dot_general(mine_rows, pick, NN, precision=lax.Precision.HIGHEST,
                                  preferred_element_type=jnp.float32)


def whole(n):
    return [pl.BlockSpec(memory_space=pltpu.VMEM)] * n


def call(kernel, shapes, in_specs, scratch, name):
    return pl.pallas_call(
        kernel,
        out_shape=[jax.ShapeDtypeStruct(s, t) for s, t in shapes],
        in_specs=in_specs,
        out_specs=whole(len(shapes)),
        scratch_shapes=scratch,
        compiler_params=pltpu.CompilerParams(vmem_limit_bytes=VMEM),
        name=name,
    )


def local(train_acts, train_grads, train_lengths, query_acts, query_grads, query_lengths,
          proj_in, proj_out):
    d, ff = proj_in.shape[1], proj_out.shape[1]
    bf, f32 = jnp.bfloat16, jnp.float32
    other_core = [(i, i ^ 1) for i in range(4)]
    other_chip = [(i, i ^ 2) for i in range(4)]
    keep, give = call(
        project_kernel,
        [((208, 128), f32)] * 2,
        [pl.BlockSpec(memory_space=pltpu.HBM)] * 6,
        [
            pltpu.VMEM((272, d), bf),
            pltpu.VMEM((272, ff), bf),
            pltpu.VMEM((64, d), bf),
            pltpu.VMEM((64, ff), bf),
            pltpu.VMEM((64, 256), f32),
            pltpu.SemaphoreType.DMA((18,)),
        ],
        "project",
    )(*(pltpu.with_memory_space_constraint(a, pltpu.HBM)
        for a in (train_acts, train_grads, query_acts.reshape(16, d),
                  query_grads.reshape(16, ff), proj_in, proj_out)))
    keep = keep + lax.ppermute(give, "mp", other_core)
    got = lax.ppermute(keep[32:], "mp", other_chip)
    smem = pl.BlockSpec(memory_space=pltpu.SMEM)
    (tiles,) = call(
        features_kernel,
        [((48, 128), f32)],
        [smem, smem] + whole(2),
        [pltpu.VMEM((64, 128), f32), pltpu.VMEM((128, 128), f32)],
        "features",
    )(train_lengths, query_lengths, keep, got)
    size = lax.axis_size("dp")
    tiles = lax.all_to_all(jnp.broadcast_to(tiles[None], (size, 48, 128)), "dp", 0, 0, tiled=True)
    part, xh, xl = call(
        gram_kernel,
        [((136, 128), f32), ((192, 1024), bf), ((192, 1024), bf)],
        whole(1),
        [],
        "gram",
    )(tiles.reshape(-1, 128))
    part = part + lax.ppermute(part, "mp", other_core)
    got = lax.ppermute(part, "mp", other_chip)
    precond, scores = call(
        solve_kernel,
        [((64, 1024), f32), ((4, 16), f32)],
        whole(4),
        [pltpu.VMEM((128, 128), f32)] * 2,
        "solve",
    )(part, got, xh, xl)
    return precond, scores


def solution(mesh):
    in_specs = (
        P("dp", None, "mp"),
        P("dp", None, "mp"),
        P("dp"),
        P("dp", None, "mp"),
        P("dp", None, "mp"),
        P("dp"),
        P(None, "mp"),
        P(None, "mp"),
    )
    out_specs = (P(None, "mp"), P("dp", "mp"))
    return jax.shard_map(local, mesh=mesh, in_specs=in_specs, out_specs=out_specs, check_vma=False)
```

time: 49.5 us -> 46.5 us (0.939)
  Pallas kernels: 8.14 us -> 6.98 us
  blocking collectives: 26.3 us -> 25.2 us
  waiting for transfers between devices: 7.91 us -> 7.2 us
    pallas_call x4, Pallas kernels: 8.14 us -> 6.98 us  [the longest x1 2.98 us: local(): call(project_kernel, [((208, 128), f32)] * 2, [pl.BlockSpec(memory_space=...]
    all_to_all x1, blocking collectives: 26.3 us -> 25.2 us  [local(): lax.all_to_all(jnp.broadcast_to(tiles[None], (size, 48, 128)), 'dp', 0, 0...]
    ppermute x6 -> x4, waiting for transfers between devices: 7.91 us -> 7.2 us  [the longest x1 2.79 us: local(): got = lax.ppermute(part, 'mp', other_chip)]
    ppermute x6 -> x4, starting transfers between devices: 6.29 us -> 6.07 us  [the longest x1 2.75 us: local(): part = part + lax.ppermute(part, 'mp', other_core)]
  transfers between devices with their start and end apart: 6 -> 4, of which waited for: 4 -> 4; matrix products, arithmetic and copies ran while one was open for 0% -> 0% of each run, Pallas kernels for 0% -> 0%
where the time goes in v3:
time: 46.5 us; the launch traced here: 46.2 us
  blocking collectives  25.2 us (54%)
  waiting for transfers between devices  7.2 us (15%)
  Pallas kernels  6.98 us (15%)
  starting transfers between devices  6.07 us (13%)
  between operations  0.69 us (1%)
    all_to_all x1, blocking collectives, local(): lax.all_to_all(jnp.broadcast_to(tiles[None], (size, 48, 128)), 'dp', 0, 0...  25.2 us
    pallas_call x1, Pallas kernels, local(): call(project_kernel, [((208, 128), f32)] * 2, [pl.BlockSpec(memory_space=...  2.98 us
    ppermute x1, waiting for transfers between devices, local(): got = lax.ppermute(part, 'mp', other_chip)  2.79 us
    ppermute x1, starting transfers between devices, local(): part = part + lax.ppermute(part, 'mp', other_core)  2.75 us
    ppermute x1, waiting for transfers between devices, local(): got = lax.ppermute(keep[32:], 'mp', other_chip)  2.55 us
    pallas_call x1, Pallas kernels, local(): call(solve_kernel, [((64, 1024), f32), ((4, 16), f32)], whole(4), [pltpu....  2.29 us
    ppermute x1, starting transfers between devices, local(): keep = keep + lax.ppermute(give, 'mp', other_core)  1.5 us
    ppermute x1, starting transfers between devices, local(): got = lax.ppermute(keep[32:], 'mp', other_chip)  1.37 us
  transfers between devices with their start and end apart: 4, of which 4 were waited for; matrix products, arithmetic and copies ran while one was open for 0% of the time, Pallas kernels for 0%

profile of v3, /device:TPU:1, one launch (start us, length us, event | category | flops | bytes accessed | tf_op | source)
XLA Modules:
  0.0 46.2 jit_solution(12143889415430307559)
XLA Ops:
  0.6 0.0 copy-start.1
  0.6 0.0 copy-start
  0.7 3.0 %project.1 = (f32[208,128]{1,0:T(8,128)S(1)}, f32[208,128]{1,0:T(8,128)S(1)}) custom-call(bf16[4,64,1024]{2,1,0:T(8,128)(2,1)} %ta.1, bf16[4,64,3584]{2,1,0:T(8,128)(2,1)} %tg.1, bf16[16,1024]{1,0:T(8,128)(2,1)} %bitcast.5, bf16[16,3584]{1,0:T(8,128)(2,1)} %bitcast.4, bf16[64,1024]{1,0:T(8,128)(2,1)} %pi.1, bf16[64,3584]{1,0:T(8,128)(2,1)} %po.1), custom_call_target="tpu_custom_call" | custom-call | tf_op jit(solution)/shard_map/project/pallas_call | solution.py:237
  3.6 1.5 %collective-permute-start = (f32[208,128]{1,0:T(8,128)S(1)}, f32[208,128]{1,0:T(8,128)S(1)}, u32[]{:S(2)}, u32[]{:S(2)}) collective-permute-start(f32[208,128]{1,0:T(8,128)S(1)} %get-tuple-element.8), channel_id=1, source_target_pairs={{0,1},{1,0},{2,3},{3,2},{4,5},{5,4},{6,7},{7,6},{8,9},{9,8},{10,11... | collective-permute-start | bytes 319496 | tf_op jit(solution)/shard_map/ppermute | solution.py:253
  5.1 1.0 %collective-permute-done = f32[208,128]{1,0:T(8,128)S(1)} collective-permute-done((f32[208,128]{1,0:T(8,128)S(1)}, f32[208,128]{1,0:T(8,128)S(1)}, u32[]{:S(2)}, u32[]{:S(2)}) %collective-permute-start) | collective-permute-done | bytes 106528 | tf_op jit(solution)/shard_map/ppermute | solution.py:253
  6.1 1.4 %collective-permute-start.1 = (f32[176,128]{1,0:T(8,128)S(1)}, f32[176,128]{1,0:T(8,128)S(1)}, u32[]{:S(2)}, u32[]{:S(2)}) collective-permute-start(f32[176,128]{1,0:T(8,128)S(1)} %slice.4), channel_id=1, source_target_pairs={{0,2},{1,3},{2,0},{3,1},{4,6},{5,7},{6,4},{7,5},{8,10},{9,11},{10,... | collective-permute-start | bytes 270344 | tf_op jit(solution)/shard_map/ppermute | solution.py:254
  7.5 2.5 %collective-permute-done.1.got = f32[176,128]{1,0:T(8,128)S(1)} collective-permute-done((f32[176,128]{1,0:T(8,128)S(1)}, f32[176,128]{1,0:T(8,128)S(1)}, u32[]{:S(2)}, u32[]{:S(2)}) %collective-permute-start.1) | collective-permute-done | bytes 90144 | tf_op jit(solution)/shard_map/ppermute | solution.py:254
  10.1 0.0 copy-done.1
  10.1 0.0 copy-done
  10.1 0.8 %features.1 = f32[48,128]{1,0:T(8,128)S(1)} custom-call(s32[4]{0:T(128)S(1)} %copy-done, s32[2]{0:T(128)S(1)} %copy-done.1, f32[208,128]{1,0:T(8,128)S(1)} %add.6.mine, f32[176,128]{1,0:T(8,128)S(1)} %collective-permute-done.1.got), custom_call_target="tpu_custom_call" | custom-call | tf_op jit(solution)/shard_map/features/pallas_call | solution.py:256
  10.9 0.1 broadcast_in_dim.2
  10.9 25.2 %all_to_all.5 = f32[32,48,128]{2,1,0:T(8,128)S(1)} all-to-all(f32[32,48,128]{2,1,0:T(8,128)S(1)} %broadcast_in_dim.2), channel_id=1, replica_groups=mesh['dp'=32,'mp'=4] {'dp'}, dimensions={0} | all-to-all | bytes 1572864 | tf_op jit(solution)/shard_map/all_to_all | solution.py:264
  36.1 0.9 %gram.1 = (f32[136,128]{1,0:T(8,128)S(1)}, bf16[192,1024]{1,0:T(8,128)(2,1)S(1)}, bf16[192,1024]{1,0:T(8,128)(2,1)S(1)}) custom-call(f32[1536,128]{1,0:T(8,128)S(1)} %bitcast.3), custom_call_target="tpu_custom_call" | custom-call | tf_op jit(solution)/shard_map/gram/pallas_call | solution.py:265
  37.0 2.7 %collective-permute-start.2 = (f32[136,128]{1,0:T(8,128)S(1)}, f32[136,128]{1,0:T(8,128)S(1)}, u32[]{:S(2)}, u32[]{:S(2)}) collective-permute-start(f32[136,128]{1,0:T(8,128)S(1)} %get-tuple-element.9), channel_id=1, source_target_pairs={{0,1},{1,0},{2,3},{3,2},{4,5},{5,4},{6,7},{7,6},{8,9},{9,8},{10,11... | collective-permute-start | bytes 208904 | tf_op jit(solution)/shard_map/ppermute | solution.py:272
  39.8 0.9 %collective-permute-done.2 = f32[136,128]{1,0:T(8,128)S(1)} collective-permute-done((f32[136,128]{1,0:T(8,128)S(1)}, f32[136,128]{1,0:T(8,128)S(1)}, u32[]{:S(2)}, u32[]{:S(2)}) %collective-permute-start.2) | collective-permute-done | bytes 69664 | tf_op jit(solution)/shard_map/ppermute | solution.py:272
  40.7 0.5 collective-permute-start.3
  41.2 2.8 %collective-permute-done.3.got = f32[136,128]{1,0:T(8,128)S(1)} collective-permute-done((f32[136,128]{1,0:T(8,128)S(1)}, f32[136,128]{1,0:T(8,128)S(1)}, u32[]{:S(2)}, u32[]{:S(2)}) %collective-permute-start.3) | collective-permute-done | bytes 69664 | tf_op jit(solution)/shard_map/ppermute | solution.py:273
  44.0 2.3 %solve.1 = (f32[64,1024]{1,0:T(8,128)}, f32[4,16]{1,0:T(4,128)}) custom-call(f32[136,128]{1,0:T(8,128)S(1)} %add.7.mine, f32[136,128]{1,0:T(8,128)S(1)} %collective-permute-done.3.got, bf16[192,1024]{1,0:T(8,128)(2,1)S(1)} %get-tuple-element.10.xh, bf16[192,1024]{1,0:T(8,128)(2,1)S(1)} %get-tuple-element.11.xl), custom_call_target="tpu_custom_call" | custom-call | tf_op jit(solution)/shard_map/solve/pallas_call | solution.py:274
  (3 shorter events, 0.0 us)
Async XLA Ops:
  0.6 9.4 %copy-start.1 = (s32[2]{0:T(128)S(1)}, s32[2]{0:T(128)}, u32[]{:S(2)}) copy-start(s32[2]{0:T(128)} %ql.1) | copy-start | bytes 28
  0.6 9.4 %copy-start = (s32[4]{0:T(128)S(1)}, s32[4]{0:T(128)}, u32[]{:S(2)}) copy-start(s32[4]{0:T(128)} %tl.1) | copy-start | bytes 52
  3.6 2.5 %collective-permute-start = (f32[208,128]{1,0:T(8,128)S(1)}, f32[208,128]{1,0:T(8,128)S(1)}, u32[]{:S(2)}, u32[]{:S(2)}) collective-permute-start(f32[208,128]{1,0:T(8,128)S(1)} %get-tuple-element.8), channel_id=1, source_target_pairs={{0,1},{1,0},{2,3},{3,2},{4,5},{5,4},{6,7},{7,6},{8,9},{9,8},{10,11... | collective-permute-start | bytes 319496 | tf_op jit(solution)/shard_map/ppermute | solution.py:253
  6.1 3.9 %collective-permute-start.1 = (f32[176,128]{1,0:T(8,128)S(1)}, f32[176,128]{1,0:T(8,128)S(1)}, u32[]{:S(2)}, u32[]{:S(2)}) collective-permute-start(f32[176,128]{1,0:T(8,128)S(1)} %slice.4), channel_id=1, source_target_pairs={{0,2},{1,3},{2,0},{3,1},{4,6},{5,7},{6,4},{7,5},{8,10},{9,11},{10,... | collective-permute-start | bytes 270344 | tf_op jit(solution)/shard_map/ppermute | solution.py:254
  37.0 3.7 %collective-permute-start.2 = (f32[136,128]{1,0:T(8,128)S(1)}, f32[136,128]{1,0:T(8,128)S(1)}, u32[]{:S(2)}, u32[]{:S(2)}) collective-permute-start(f32[136,128]{1,0:T(8,128)S(1)} %get-tuple-element.9), channel_id=1, source_target_pairs={{0,1},{1,0},{2,3},{3,2},{4,5},{5,4},{6,7},{7,6},{8,9},{9,8},{10,11... | collective-permute-start | bytes 208904 | tf_op jit(solution)/shard_map/ppermute | solution.py:272
  40.7 3.2 %collective-permute-start.3 = (f32[136,128]{1,0:T(8,128)S(1)}, f32[136,128]{1,0:T(8,128)S(1)}, u32[]{:S(2)}, u32[]{:S(2)}) collective-permute-start(f32[136,128]{1,0:T(8,128)S(1)} %add.7.mine), channel_id=1, source_target_pairs={{0,2},{1,3},{2,0},{3,1},{4,6},{5,7},{6,4},{7,5},{8,10},{9,11},{10,... | collective-permute-start | bytes 208904 | tf_op jit(solution)/shard_map/ppermute | solution.py:273

commit v4 on v3

v4 whole, which is shorter than its diff:
```python
import math

import jax
import jax.numpy as jnp
from jax import lax
from jax.experimental import pallas as pl
from jax.experimental.pallas import tpu as pltpu
from jax.sharding import PartitionSpec as P

ITERS = 4
DAMPING = 0.5
EPSILON = 1e-06
ROWS, QUERIES, RANK, LEN, QLEN = 128, 64, 64, 64, 8
VMEM = 48 * 2**20

NT = (((1,), (1,)), ((), ()))
NN = (((1,), (0,)), ((), ()))
TN = (((0,), (0,)), ((), ()))


def mm(a, b, dims):
    return lax.dot_general(a, b, dims, preferred_element_type=jnp.float32)


def split(x):
    high = x.astype(jnp.bfloat16)
    return high, (x - high.astype(jnp.float32)).astype(jnp.bfloat16)


def project_kernel(tl, ql, ta, tg, qa, qg, pi, po, keep, give,
                   tl_s, ql_s, a_v, g_v, pi_v, po_v, out_t, sems):
    slots, ff = tg.shape
    bounds = (0, 1280, 2560, 3584)
    count = iter(range(32))

    def load(src, dst):
        return pltpu.make_async_copy(src, dst, sems.at[next(count)])

    groups = [[load(pi, pi_v), load(qa, a_v.at[slots : slots + 16]), load(ta, a_v.at[0:slots])]]
    for lo, hi in zip(bounds[:-1], bounds[1:]):
        cols = pl.ds(lo, hi - lo)
        groups.append([load(po.at[:, cols], po_v.at[:, cols]),
                       load(qg.at[:, cols], g_v.at[slots : slots + 16, cols]),
                       load(tg.at[:, cols], g_v.at[0:slots, cols])])
    groups.append([load(tl, tl_s), load(ql, ql_s)])
    for group in groups:
        for c in group:
            c.start()
    me = lax.axis_index("mp")
    for c in groups[0]:
        c.wait()
    inn = mm(a_v[...], pi_v[...], NT)
    train_in = inn[0:slots].T
    for o in (keep, give):
        o[32:96, :] = train_in[:, 0:128]
        o[96:160, :] = train_in[:, 128:256]
    out = None
    for k in range(len(bounds) - 1):
        for c in groups[k + 1]:
            c.wait()
        cols = slice(bounds[k], bounds[k + 1])
        term = mm(g_v[:, cols], po_v[:, cols], NT)
        out = term if out is None else out + term
    for c in groups[-1]:
        c.wait()
    slot = lax.broadcasted_iota(jnp.int32, (16, 64), 0)
    used = slot < jnp.minimum(ql_s[0], QLEN)
    used |= (slot >= QLEN) & (slot < QLEN + ql_s[1])
    queries = jnp.concatenate([inn[slots:], jnp.where(used, out[slots:], 0.0)], axis=1)
    lane = lax.broadcasted_iota(jnp.int32, (64, slots), 1)
    used = None
    for r in range(slots // LEN):
        own = (lane >= LEN * r) & (lane < LEN * r + jnp.minimum(tl_s[r], LEN))
        used = own if used is None else used | own
    out_t[...] = jnp.where(used, out[0:slots].T, 0.0)
    for core, o in enumerate((keep, give)):
        o[160:176, :] = queries
        for chip, at in enumerate((0, 176)):
            who = me ^ (core + 2 * chip)
            quarter = out_t[pl.ds(pl.multiple_of(who * 16, 16), 16), :]
            o[at : at + 16, :] = quarter[:, 0:128]
            o[at + 16 : at + 32, :] = quarter[:, 128:256]


def dot3(a, b, axis):
    ah, al = split(a)
    bh, bl = split(b)
    dims = NT if axis == 1 else TN
    return mm(jnp.concatenate([ah, ah, al], axis=axis), jnp.concatenate([bh, bl, bh], axis=axis), dims)


def features_kernel(mine, got, feats, scr, qscr):
    me = lax.axis_index("mp")
    left_lanes = lax.broadcasted_iota(jnp.int32, (16, 128), 1) < 64
    low = left_lanes[0:8]
    q = mine[160:176] + got[128:144]
    early = lax.broadcasted_iota(jnp.int32, (16, 64), 0) < QLEN
    qin, qout = q[:, 0:64], q[:, 64:128]
    left = jnp.concatenate([jnp.where(early, qout, 0.0), jnp.where(early, 0.0, qout)], axis=1)
    qscr[...] = dot3(left, jnp.concatenate([qin, qin], axis=1), 0)
    for pair in range(2):
        out = mine[16 * pair : 16 * pair + 16] + got[144 + 16 * pair : 160 + 16 * pair]
        inn = mine[32 + 64 * pair : 96 + 64 * pair] + got[64 * pair : 64 * pair + 64]
        left = jnp.concatenate([jnp.where(left_lanes, out, 0.0), jnp.where(left_lanes, 0.0, out)], axis=0)
        scr[32 * pair : 32 * pair + 32, :] = dot3(left, jnp.concatenate([inn, inn], axis=0), 1)
    for r in range(2):
        scr[64 + 16 * r : 80 + 16 * r, :] = qscr[pl.ds(pl.multiple_of(64 * r + me * 16, 16), 16), :]
    for r in range(6):
        even = scr[pl.ds(16 * r, 8, stride=2), :]
        odd = scr[pl.ds(16 * r + 1, 8, stride=2), :]
        scale = 1.0 / math.sqrt(LEN if r < 4 else QLEN)
        feats[8 * r : 8 * r + 8, :] = jnp.where(low, even, odd) * scale


def gram_kernel(tiles, part, xh_ref, xl_ref):
    squares = jnp.zeros((64, 128), jnp.float32)
    total = None
    for base in range(0, 8, 2):
        highs, lows = [], []
        for a in range(base, base + 2):
            x = jnp.concatenate([tiles[pl.ds(8 * r + a, 32, stride=48), :] for r in range(6)], axis=0)
            squares += x[128:192] * x[128:192]
            high, low = split(x)
            xh_ref[:, 128 * a : 128 * a + 128] = high
            xl_ref[:, 128 * a : 128 * a + 128] = low
            highs.append(high)
            lows.append(low)
        high = jnp.concatenate(highs, axis=1)
        low = jnp.concatenate(lows, axis=1)
        t = mm(jnp.concatenate([high[0:128], low[0:128]], axis=0), high, NT)
        term = t[0:128] + t[128:256] + mm(high[0:128], low, NT)
        total = term if total is None else total + term
    ones = jnp.ones((16, 128), jnp.bfloat16)
    high, low = split(squares)
    norms = mm(ones, high, NT) + mm(ones, low, NT)
    row = lax.broadcasted_iota(jnp.int32, (64, 64), 0)
    col = lax.broadcasted_iota(jnp.int32, (64, 64), 1)
    first = total[0:64, 0:64]
    both = jnp.where(row >= col, total[64:128, 64:128], first)
    part[0:64, :] = jnp.concatenate([total[64:128, 0:64], both], axis=1)
    part[64:128, :] = jnp.concatenate([total[0:64, 128:192], total[64:128, 128:192]], axis=1)
    diag = jnp.sum(jnp.where(row == col, first, 0.0), axis=0, keepdims=True)
    part[128:136, :] = jnp.concatenate([norms[0:8], jnp.broadcast_to(diag, (8, 64))], axis=1)


def solve_kernel(mine, got, xh, xl, precond, scores, ys, ts, zs, sems):
    dp = lax.axis_index("dp")
    me = lax.axis_index("mp")
    x = mine[...] + got[...]
    row = lax.broadcasted_iota(jnp.int32, (64, 64), 0)
    col = lax.broadcasted_iota(jnp.int32, (64, 64), 1)
    corner, both = x[0:64, 0:64], x[0:64, 64:128]
    flip = both.T
    diag = x[128:129, 64:128]
    upper = jnp.where(row < col, both, jnp.where(row > col, flip, diag))
    lower = jnp.where(row < col, flip, both)
    gram = jnp.concatenate(
        [jnp.concatenate([upper, corner.T], axis=1), jnp.concatenate([corner, lower], axis=1)],
        axis=0,
    )
    cross = jnp.concatenate([x[64:128, 0:64], x[64:128, 64:128]], axis=0)
    norm_q = x[128:129, 0:64]
    trace = jnp.sum(diag + jnp.sum(jnp.where(row == col, both, 0.0), axis=0, keepdims=True),
                    axis=1, keepdims=True)
    damp = trace * (DAMPING / (ROWS * RANK * RANK)) + EPSILON
    inv_rows = 1.0 / ROWS
    gh, gl = split(gram)
    spread = jnp.concatenate([gh, gl, gh], axis=1)

    def times_gram(y):
        yh, yl = split(y)
        return mm(spread, jnp.concatenate([yh, yh, yl], axis=0), NN)

    def total(v):
        return jnp.sum(v, axis=0, keepdims=True)

    def inner(alpha, w, y):
        return alpha * alpha * norm_q + total(w * (alpha * cross + y))

    rr = norm_q
    size = rr / (damp * rr + total(cross * cross) * inv_rows)
    za, zw, zy = size, jnp.zeros_like(cross), size * cross
    ra, rw = 1.0 - size * damp, (-inv_rows * size) * cross
    ry = cross - size * (damp * cross + times_gram(cross) * inv_rows)
    new = inner(ra, rw, ry)
    ratio = new / rr
    da, dw, dy = ra + ratio, rw, ry + ratio * cross
    for step in range(1, ITERS):
        rr = new
        curvature = damp * inner(da, dw, dy) + total(dy * dy) * inv_rows
        size = rr / curvature
        za, zw, zy = za + size * da, zw + size * dw, zy + size * dy
        if step == ITERS - 1:
            break
        iy = damp * dy + times_gram(dy) * inv_rows
        ra = ra - size * (damp * da)
        rw = rw - size * (damp * dw + dy * inv_rows)
        ry = ry - size * iy
        new = inner(ra, rw, ry)
        ratio = new / rr
        da, dw, dy = ra + ratio * da, rw + ratio * dw, ry + ratio * dy
    weights = jnp.concatenate([zw, jnp.where(row == col, za, 0.0)], axis=0)
    turned = weights.T
    pad = jnp.zeros((32, 64), jnp.float32)
    for k in range(2):
        turn = turned[32 * k : 32 * k + 32]
        ts[pl.ds(k, 32, stride=2), :] = turn[:, 0:128]
        ts[pl.ds(64 + k, 32, stride=2), :] = jnp.concatenate([turn[:, 128:192], pad], axis=1)
    wh, wl = split(jnp.concatenate([ts[0:64, :], ts[64:128, 0:64]], axis=1))
    ys[...] = jnp.concatenate([zy, jnp.zeros_like(zy)], axis=1)
    stacked = jnp.concatenate([wh, wl], axis=0)
    width = 512
    copies = []
    for c in range(2):
        cols = slice(width * c, width * (c + 1))
        z = mm(stacked, xh[:, cols], NN)
        precond[:, cols] = z[0:64] + z[64:128] + mm(wh, xl[:, cols], NN)
    mine_rows = ys[pl.ds(dp, 4, stride=32), :][:, 0:64]
    slot = lax.broadcasted_iota(jnp.int32, (64, 16), 0)
    want = lax.broadcasted_iota(jnp.int32, (64, 16), 1)
    pick = (slot == (want % 2) * 32 + 8 * me + want // 2).astype(jnp.float32)
    scores[...] = lax.dot_general(mine_rows, pick, NN, precision=lax.Precision.HIGHEST,
                                  preferred_element_type=jnp.float32)


def whole(n):
    return [pl.BlockSpec(memory_space=pltpu.VMEM)] * n


def call(kernel, shapes, in_specs, scratch, name, out_specs=None):
    return pl.pallas_call(
        kernel,
        out_shape=[jax.ShapeDtypeStruct(s, t) for s, t in shapes],
        in_specs=in_specs,
        out_specs=out_specs or whole(len(shapes)),
        scratch_shapes=scratch,
        compiler_params=pltpu.CompilerParams(vmem_limit_bytes=VMEM),
        name=name,
    )


def local(train_acts, train_grads, train_lengths, query_acts, query_grads, query_lengths,
          proj_in, proj_out):
    d, ff = proj_in.shape[1], proj_out.shape[1]
    bf, f32 = jnp.bfloat16, jnp.float32
    other_core = [(i, i ^ 1) for i in range(4)]
    other_chip = [(i, i ^ 2) for i in range(4)]
    keep, give = call(
        project_kernel,
        [((208, 128), f32)] * 2,
        [pl.BlockSpec(memory_space=pltpu.HBM)] * 8,
        [
            pltpu.SMEM((4,), jnp.int32),
            pltpu.SMEM((2,), jnp.int32),
            pltpu.VMEM((272, d), bf),
            pltpu.VMEM((272, ff), bf),
            pltpu.VMEM((64, d), bf),
            pltpu.VMEM((64, ff), bf),
            pltpu.VMEM((64, 256), f32),
            pltpu.SemaphoreType.DMA((18,)),
        ],
        "project",
    )(*(pltpu.with_memory_space_constraint(a, pltpu.HBM)
        for a in (train_lengths, query_lengths, train_acts.reshape(256, d), train_grads.reshape(256, ff), query_acts.reshape(16, d),
                  query_grads.reshape(16, ff), proj_in, proj_out)))
    keep = keep + lax.ppermute(give, "mp", other_core)
    got = lax.ppermute(keep[32:], "mp", other_chip)
    (tiles,) = call(
        features_kernel,
        [((48, 128), f32)],
        whole(2),
        [pltpu.VMEM((96, 128), f32), pltpu.VMEM((128, 128), f32)],
        "features",
    )(keep, got)
    size = lax.axis_size("dp")
    tiles = lax.all_to_all(jnp.broadcast_to(tiles[None], (size, 48, 128)), "dp", 0, 0, tiled=True)
    part, xh, xl = call(
        gram_kernel,
        [((136, 128), f32), ((192, 1024), bf), ((192, 1024), bf)],
        whole(1),
        [],
        "gram",
    )(tiles.reshape(-1, 128))
    part = part + lax.ppermute(part, "mp", other_core)
    got = lax.ppermute(part, "mp", other_chip)
    precond, scores = call(
        solve_kernel,
        [((64, 1024), f32), ((4, 16), f32)],
        whole(4),
        [pltpu.VMEM((128, 128), f32), pltpu.VMEM((128, 128), f32),
         pltpu.VMEM((64, 1024), f32), pltpu.SemaphoreType.DMA((2,))],
        "solve",
    )(part, got, xh, xl)
    return precond, scores


def solution(mesh):
    in_specs = (
        P("dp", None, "mp"),
        P("dp", None, "mp"),
        P("dp"),
        P("dp", None, "mp"),
        P("dp", None, "mp"),
        P("dp"),
        P(None, "mp"),
        P(None, "mp"),
    )
    out_specs = (P(None, "mp"), P("dp", "mp"))
    return jax.shard_map(local, mesh=mesh, in_specs=in_specs, out_specs=out_specs, check_vma=False)
```

time: 46.5 us -> 45.4 us (0.976)
  Pallas kernels: 6.98 us -> 5.87 us
    pallas_call x1, Pallas kernels: 0.81 us -> 0.31 us  [local(): call(features_kernel, [((48, 128), f32)], whole(2), [pltpu.VMEM((96, 128)...]
where the time goes in v4:
time: 45.4 us; the launch traced here: 45.1 us
  blocking collectives  25.2 us (56%)
  waiting for transfers between devices  7.21 us (16%)
  starting transfers between devices  6.06 us (13%)
  Pallas kernels  5.87 us (13%)
  between operations  0.67 us (1%)
    all_to_all x1, blocking collectives, local(): lax.all_to_all(jnp.broadcast_to(tiles[None], (size, 48, 128)), 'dp', 0, 0...  25.2 us
    pallas_call x1, Pallas kernels, local(): call(project_kernel, [((208, 128), f32)] * 2, [pl.BlockSpec(memory_space=...  2.88 us
    ppermute x1, waiting for transfers between devices, local(): got = lax.ppermute(part, 'mp', other_chip)  2.8 us
    ppermute x1, starting transfers between devices, local(): part = part + lax.ppermute(part, 'mp', other_core)  2.75 us
    ppermute x1, waiting for transfers between devices, local(): got = lax.ppermute(keep[32:], 'mp', other_chip)  2.55 us
    pallas_call x1, Pallas kernels, local(): call(solve_kernel, [((64, 1024), f32), ((4, 16), f32)], whole(4), [pltpu....  2 us
    ppermute x1, starting transfers between devices, local(): keep = keep + lax.ppermute(give, 'mp', other_core)  1.5 us
    ppermute x1, starting transfers between devices, local(): got = lax.ppermute(keep[32:], 'mp', other_chip)  1.37 us
  transfers between devices with their start and end apart: 4, of which 4 were waited for; matrix products, arithmetic and copies ran while one was open for 0% of the time, Pallas kernels for 0%

profile of v4, /device:TPU:1, one launch (start us, length us, event | category | flops | bytes accessed | tf_op | source)
XLA Modules:
  0.0 45.1 jit_solution(2751758482832638301)
XLA Ops:
  0.6 2.9 %project.1 = (f32[208,128]{1,0:T(8,128)S(1)}, f32[208,128]{1,0:T(8,128)S(1)}) custom-call(s32[4]{0:T(128)} %tl.1, s32[2]{0:T(128)} %ql.1, bf16[256,1024]{1,0:T(8,128)(2,1)} %bitcast.7, bf16[256,3584]{1,0:T(8,128)(2,1)} %bitcast.6, bf16[16,1024]{1,0:T(8,128)(2,1)} %bitcast.9, bf16[16,3584]{1,0:T(8,128)(2,1)} %bitcast.8, bf16[64,1024]{1,0:T(8,128)(2,1)} %pi.1, ...), custom_call_target="tpu_custom_call" | custom-call | tf_op jit(solution)/shard_map/project/pallas_call | solution.py:248
  3.5 1.5 %collective-permute-start = (f32[208,128]{1,0:T(8,128)S(1)}, f32[208,128]{1,0:T(8,128)S(1)}, u32[]{:S(2)}, u32[]{:S(2)}) collective-permute-start(f32[208,128]{1,0:T(8,128)S(1)} %get-tuple-element.8), channel_id=1, source_target_pairs={{0,1},{1,0},{2,3},{3,2},{4,5},{5,4},{6,7},{7,6},{8,9},{9,8},{10,11... | collective-permute-start | bytes 319496 | tf_op jit(solution)/shard_map/ppermute | solution.py:266
  5.0 1.0 %collective-permute-done = f32[208,128]{1,0:T(8,128)S(1)} collective-permute-done((f32[208,128]{1,0:T(8,128)S(1)}, f32[208,128]{1,0:T(8,128)S(1)}, u32[]{:S(2)}, u32[]{:S(2)}) %collective-permute-start) | collective-permute-done | bytes 106528 | tf_op jit(solution)/shard_map/ppermute | solution.py:266
  6.0 1.4 %collective-permute-start.1 = (f32[176,128]{1,0:T(8,128)S(1)}, f32[176,128]{1,0:T(8,128)S(1)}, u32[]{:S(2)}, u32[]{:S(2)}) collective-permute-start(f32[176,128]{1,0:T(8,128)S(1)} %slice.4), channel_id=1, source_target_pairs={{0,2},{1,3},{2,0},{3,1},{4,6},{5,7},{6,4},{7,5},{8,10},{9,11},{10,... | collective-permute-start | bytes 270344 | tf_op jit(solution)/shard_map/ppermute | solution.py:267
  7.4 2.5 %collective-permute-done.1.got = f32[176,128]{1,0:T(8,128)S(1)} collective-permute-done((f32[176,128]{1,0:T(8,128)S(1)}, f32[176,128]{1,0:T(8,128)S(1)}, u32[]{:S(2)}, u32[]{:S(2)}) %collective-permute-start.1) | collective-permute-done | bytes 90144 | tf_op jit(solution)/shard_map/ppermute | solution.py:267
  9.9 0.3 features.1
  10.2 0.1 broadcast_in_dim.2
  10.3 25.2 %all_to_all.5 = f32[32,48,128]{2,1,0:T(8,128)S(1)} all-to-all(f32[32,48,128]{2,1,0:T(8,128)S(1)} %broadcast_in_dim.2), channel_id=1, replica_groups=mesh['dp'=32,'mp'=4] {'dp'}, dimensions={0} | all-to-all | bytes 1572864 | tf_op jit(solution)/shard_map/all_to_all | solution.py:276
  35.5 0.7 %gram.1 = (f32[136,128]{1,0:T(8,128)S(1)}, bf16[192,1024]{1,0:T(8,128)(2,1)S(1)}, bf16[192,1024]{1,0:T(8,128)(2,1)S(1)}) custom-call(f32[1536,128]{1,0:T(8,128)S(1)} %bitcast.5), custom_call_target="tpu_custom_call" | custom-call | tf_op jit(solution)/shard_map/gram/pallas_call | solution.py:277
  36.2 2.7 %collective-permute-start.2 = (f32[136,128]{1,0:T(8,128)S(1)}, f32[136,128]{1,0:T(8,128)S(1)}, u32[]{:S(2)}, u32[]{:S(2)}) collective-permute-start(f32[136,128]{1,0:T(8,128)S(1)} %get-tuple-element.9), channel_id=1, source_target_pairs={{0,1},{1,0},{2,3},{3,2},{4,5},{5,4},{6,7},{7,6},{8,9},{9,8},{10,11... | collective-permute-start | bytes 208904 | tf_op jit(solution)/shard_map/ppermute | solution.py:284
  39.0 0.9 %collective-permute-done.2 = f32[136,128]{1,0:T(8,128)S(1)} collective-permute-done((f32[136,128]{1,0:T(8,128)S(1)}, f32[136,128]{1,0:T(8,128)S(1)}, u32[]{:S(2)}, u32[]{:S(2)}) %collective-permute-start.2) | collective-permute-done | bytes 69664 | tf_op jit(solution)/shard_map/ppermute | solution.py:284
  39.9 0.4 collective-permute-start.3
  40.3 2.8 %collective-permute-done.3.got = f32[136,128]{1,0:T(8,128)S(1)} collective-permute-done((f32[136,128]{1,0:T(8,128)S(1)}, f32[136,128]{1,0:T(8,128)S(1)}, u32[]{:S(2)}, u32[]{:S(2)}) %collective-permute-start.3) | collective-permute-done | bytes 69664 | tf_op jit(solution)/shard_map/ppermute | solution.py:285
  43.1 2.0 %solve.1 = (f32[64,1024]{1,0:T(8,128)}, f32[4,16]{1,0:T(4,128)}) custom-call(f32[136,128]{1,0:T(8,128)S(1)} %add.7.mine, f32[136,128]{1,0:T(8,128)S(1)} %collective-permute-done.3.got, bf16[192,1024]{1,0:T(8,128)(2,1)S(1)} %get-tuple-element.10.xh, bf16[192,1024]{1,0:T(8,128)(2,1)S(1)} %get-tuple-element.11.xl), custom_call_target="tpu_custom_call" | custom-call | tf_op jit(solution)/shard_map/solve/pallas_call | solution.py:286
  (3 shorter events, 0.0 us)
Async XLA Ops:
  3.5 2.5 %collective-permute-start = (f32[208,128]{1,0:T(8,128)S(1)}, f32[208,128]{1,0:T(8,128)S(1)}, u32[]{:S(2)}, u32[]{:S(2)}) collective-permute-start(f32[208,128]{1,0:T(8,128)S(1)} %get-tuple-element.8), channel_id=1, source_target_pairs={{0,1},{1,0},{2,3},{3,2},{4,5},{5,4},{6,7},{7,6},{8,9},{9,8},{10,11... | collective-permute-start | bytes 319496 | tf_op jit(solution)/shard_map/ppermute | solution.py:266
  6.0 3.9 %collective-permute-start.1 = (f32[176,128]{1,0:T(8,128)S(1)}, f32[176,128]{1,0:T(8,128)S(1)}, u32[]{:S(2)}, u32[]{:S(2)}) collective-permute-start(f32[176,128]{1,0:T(8,128)S(1)} %slice.4), channel_id=1, source_target_pairs={{0,2},{1,3},{2,0},{3,1},{4,6},{5,7},{6,4},{7,5},{8,10},{9,11},{10,... | collective-permute-start | bytes 270344 | tf_op jit(solution)/shard_map/ppermute | solution.py:267
  36.2 3.7 %collective-permute-start.2 = (f32[136,128]{1,0:T(8,128)S(1)}, f32[136,128]{1,0:T(8,128)S(1)}, u32[]{:S(2)}, u32[]{:S(2)}) collective-permute-start(f32[136,128]{1,0:T(8,128)S(1)} %get-tuple-element.9), channel_id=1, source_target_pairs={{0,1},{1,0},{2,3},{3,2},{4,5},{5,4},{6,7},{7,6},{8,9},{9,8},{10,11... | collective-permute-start | bytes 208904 | tf_op jit(solution)/shard_map/ppermute | solution.py:284
  39.9 3.2 %collective-permute-start.3 = (f32[136,128]{1,0:T(8,128)S(1)}, f32[136,128]{1,0:T(8,128)S(1)}, u32[]{:S(2)}, u32[]{:S(2)}) collective-permute-start(f32[136,128]{1,0:T(8,128)S(1)} %add.7.mine), channel_id=1, source_target_pairs={{0,2},{1,3},{2,0},{3,1},{4,6},{5,7},{6,4},{7,5},{8,10},{9,11},{10,... | collective-permute-start | bytes 208904 | tf_op jit(solution)/shard_map/ppermute | solution.py:285

commit v5 on v4

--- a/solution.py
+++ b/solution.py
@@ -113,12 +113,15 @@
 
 
 def gram_kernel(tiles, part, xh_ref, xl_ref):
+    planes = [tiles.at[pl.ds(384 * k, 384), :] for k in (0, 2, 1, 3)]
     squares = jnp.zeros((64, 128), jnp.float32)
     total = None
     for base in range(0, 8, 2):
         highs, lows = [], []
         for a in range(base, base + 2):
-            x = jnp.concatenate([tiles[pl.ds(8 * r + a, 32, stride=48), :] for r in range(6)], axis=0)
+            x = jnp.concatenate(
+                [p[pl.ds(8 * r + a, 8, stride=48), :] for r in range(6) for p in planes], axis=0
+            )
             squares += x[128:192] * x[128:192]
             high, low = split(x)
             xh_ref[:, 128 * a : 128 * a + 128] = high
@@ -143,7 +146,16 @@
     part[128:136, :] = jnp.concatenate([norms[0:8], jnp.broadcast_to(diag, (8, 64))], axis=1)
 
 
-def solve_kernel(mine, got, xh, xl, precond, scores, ys, ts, zs, sems):
+def query_at(i, dp):
+    slot = i & 31
+    back = (slot & 2) | ((slot >> 2) & 1)
+    z = ((dp >> 3) - back) & 3
+    y = (((dp >> 1) & 3) - (slot >> 3)) & 3
+    x = (dp & 1) ^ (slot & 1)
+    return 2 * (8 * z + 2 * y + x) + (i >> 5)
+
+
+def solve_kernel(mine, got, xh, xl, precond, scores, ys):
     dp = lax.axis_index("dp")
     me = lax.axis_index("mp")
     x = mine[...] + got[...]
@@ -200,25 +212,20 @@
         ratio = new / rr
         da, dw, dy = ra + ratio * da, rw + ratio * dw, ry + ratio * dy
     weights = jnp.concatenate([zw, jnp.where(row == col, za, 0.0)], axis=0)
-    turned = weights.T
-    pad = jnp.zeros((32, 64), jnp.float32)
-    for k in range(2):
-        turn = turned[32 * k : 32 * k + 32]
-        ts[pl.ds(k, 32, stride=2), :] = turn[:, 0:128]
-        ts[pl.ds(64 + k, 32, stride=2), :] = jnp.concatenate([turn[:, 128:192], pad], axis=1)
-    wh, wl = split(jnp.concatenate([ts[0:64, :], ts[64:128, 0:64]], axis=1))
+    place = query_at(lax.broadcasted_iota(jnp.int32, (64, 64), 1), dp)
+    order = (place == row).astype(jnp.bfloat16)
+    wh, wl = (mm(order, w, NT).astype(jnp.bfloat16) for w in split(weights))
     ys[...] = jnp.concatenate([zy, jnp.zeros_like(zy)], axis=1)
     stacked = jnp.concatenate([wh, wl], axis=0)
     width = 512
-    copies = []
     for c in range(2):
         cols = slice(width * c, width * (c + 1))
         z = mm(stacked, xh[:, cols], NN)
         precond[:, cols] = z[0:64] + z[64:128] + mm(wh, xl[:, cols], NN)
-    mine_rows = ys[pl.ds(dp, 4, stride=32), :][:, 0:64]
-    slot = lax.broadcasted_iota(jnp.int32, (64, 16), 0)
-    want = lax.broadcasted_iota(jnp.int32, (64, 16), 1)
-    pick = (slot == (want % 2) * 32 + 8 * me + want // 2).astype(jnp.float32)
+    mine_rows = ys[pl.ds(0, 4, stride=32), :][:, 0:64]
+    place = query_at(lax.broadcasted_iota(jnp.int32, (64, 16), 0), dp)
+    want = 16 * me + lax.broadcasted_iota(jnp.int32, (64, 16), 1)
+    pick = (place == want).astype(jnp.float32)
     scores[...] = lax.dot_general(mine_rows, pick, NN, precision=lax.Precision.HIGHEST,
                                   preferred_element_type=jnp.float32)
 
@@ -237,6 +244,19 @@
         compiler_params=pltpu.CompilerParams(vmem_limit_bytes=VMEM),
         name=name,
     )
+
+
+def shifts(array, step, size):
+    pieces = {0: array}
+    for k in (2, 1, 3) if size == 4 else (1,):
+        pairs = []
+        for i in range(32):
+            z, y, x = i >> 3, (i >> 1) & 3, i & 1
+            for _ in range(k):
+                z, y, x = step(z, y, x)
+            pairs.append((i, 8 * z + 2 * y + x))
+        pieces[k] = lax.ppermute(array, "dp", pairs)
+    return [pieces[k] for k in range(size)]
 
 
 def local(train_acts, train_grads, train_lengths, query_acts, query_grads, query_lengths,
@@ -272,23 +292,25 @@
         [pltpu.VMEM((96, 128), f32), pltpu.VMEM((128, 128), f32)],
         "features",
     )(keep, got)
-    size = lax.axis_size("dp")
-    tiles = lax.all_to_all(jnp.broadcast_to(tiles[None], (size, 48, 128)), "dp", 0, 0, tiled=True)
+    tiles = jnp.concatenate(shifts(tiles, lambda z, y, x: (z, y, x ^ 1), 2), axis=0)
+    t0, t1, t2, t3 = shifts(tiles, lambda z, y, x: ((z + 1) % 4, y, x), 4)
+    tiles = jnp.concatenate([t0, t2, t1, t3], axis=0)
+    p0, p1, p2, p3 = shifts(tiles, lambda z, y, x: (z, (y + 1) % 4, x), 4)
+    tiles = jnp.concatenate([p0, p2, p1, p3], axis=0)
     part, xh, xl = call(
         gram_kernel,
         [((136, 128), f32), ((192, 1024), bf), ((192, 1024), bf)],
         whole(1),
         [],
         "gram",
-    )(tiles.reshape(-1, 128))
+    )(tiles)
     part = part + lax.ppermute(part, "mp", other_core)
     got = lax.ppermute(part, "mp", other_chip)
     precond, scores = call(
         solve_kernel,
         [((64, 1024), f32), ((4, 16), f32)],
         whole(4),
-        [pltpu.VMEM((128, 128), f32), pltpu.VMEM((128, 128), f32),
-         pltpu.VMEM((64, 1024), f32), pltpu.SemaphoreType.DMA((2,))],
+        [pltpu.VMEM((128, 128), f32)],
         "solve",
     )(part, got, xh, xl)
     return precond, scores

time: 45.4 us -> 43.7 us (0.963)
  blocking collectives: 25.2 us -> 0 us
  starting transfers between devices: 6.06 us -> 21.6 us
  waiting for transfers between devices: 7.21 us -> 15 us
    all_to_all x1 -> x0, blocking collectives: 25.2 us -> none  [local(): lax.all_to_all(jnp.broadcast_to(tiles[None], (size, 48, 128)), 'dp', 0, 0...]
    ppermute x0 -> x7, starting transfers between devices: none -> 14.9 us  [shifts(): pieces[k] = lax.ppermute(array, 'dp', pairs)]
    ppermute x0 -> x7, waiting for transfers between devices: none -> 8.62 us  [shifts(): pieces[k] = lax.ppermute(array, 'dp', pairs)]
    ppermute x1, waiting for transfers between devices: 2.8 us -> 1.95 us  [local(): got = lax.ppermute(part, 'mp', other_chip)]
    ppermute x1, starting transfers between devices: 0.44 us -> 1.29 us  [local(): got = lax.ppermute(part, 'mp', other_chip)]
  transfers between devices with their start and end apart: 4 -> 11, of which waited for: 4 -> 8; matrix products, arithmetic and copies ran while one was open for 0% -> 0% of each run, Pallas kernels for 0% -> 0%
where the time goes in v5:
time: 43.7 us; the launch traced here: 43.4 us
  starting transfers between devices  21.6 us (49%)
  waiting for transfers between devices  15 us (34%)
  Pallas kernels  5.95 us (14%)
  between operations  0.72 us (2%)
    ppermute x7, starting transfers between devices, shifts(): pieces[k] = lax.ppermute(array, 'dp', pairs)  14.9 us
    ppermute x7, waiting for transfers between devices, shifts(): pieces[k] = lax.ppermute(array, 'dp', pairs)  8.62 us
    pallas_call x1, Pallas kernels, local(): call(project_kernel, [((208, 128), f32)] * 2, [pl.BlockSpec(memory_space=...  2.88 us
    ppermute x1, starting transfers between devices, local(): part = part + lax.ppermute(part, 'mp', other_core)  2.56 us
    ppermute x1, waiting for transfers between devices, local(): got = lax.ppermute(keep[32:], 'mp', other_chip)  2.55 us
    pallas_call x1, Pallas kernels, local(): call(solve_kernel, [((64, 1024), f32), ((4, 16), f32)], whole(4), [pltpu....  2.06 us
    ppermute x1, waiting for transfers between devices, local(): got = lax.ppermute(part, 'mp', other_chip)  1.95 us
    ppermute x1, starting transfers between devices, local(): keep = keep + lax.ppermute(give, 'mp', other_core)  1.5 us
  transfers between devices with their start and end apart: 11, of which 8 were waited for; matrix products, arithmetic and copies ran while one was open for 0% of the time, Pallas kernels for 0%

profile of v5, /device:TPU:1, one launch (start us, length us, event | category | flops | bytes accessed | tf_op | source)
XLA Modules:
  0.0 43.4 jit_solution(11121337504473790096)
XLA Ops:
  0.6 2.9 %project.1 = (f32[208,128]{1,0:T(8,128)S(1)}, f32[208,128]{1,0:T(8,128)S(1)}) custom-call(s32[4]{0:T(128)} %tl.1, s32[2]{0:T(128)} %ql.1, bf16[256,1024]{1,0:T(8,128)(2,1)} %bitcast.5, bf16[256,3584]{1,0:T(8,128)(2,1)} %bitcast.4, bf16[16,1024]{1,0:T(8,128)(2,1)} %bitcast.7, bf16[16,3584]{1,0:T(8,128)(2,1)} %bitcast.6, bf16[64,1024]{1,0:T(8,128)(2,1)} %pi.1, ...), custom_call_target="tpu_custom_call" | custom-call | tf_op jit(solution)/shard_map/project/pallas_call | solution.py:268
  3.5 1.5 %collective-permute-start = (f32[208,128]{1,0:T(8,128)S(1)}, f32[208,128]{1,0:T(8,128)S(1)}, u32[]{:S(2)}, u32[]{:S(2)}) collective-permute-start(f32[208,128]{1,0:T(8,128)S(1)} %get-tuple-element.8), channel_id=1, source_target_pairs={{0,1},{1,0},{2,3},{3,2},{4,5},{5,4},{6,7},{7,6},{8,9},{9,8},{10,11... | collective-permute-start | bytes 319496 | tf_op jit(solution)/shard_map/ppermute | solution.py:286
  5.0 1.0 %collective-permute-done = f32[208,128]{1,0:T(8,128)S(1)} collective-permute-done((f32[208,128]{1,0:T(8,128)S(1)}, f32[208,128]{1,0:T(8,128)S(1)}, u32[]{:S(2)}, u32[]{:S(2)}) %collective-permute-start) | collective-permute-done | bytes 106528 | tf_op jit(solution)/shard_map/ppermute | solution.py:286
  6.0 1.4 %collective-permute-start.1 = (f32[176,128]{1,0:T(8,128)S(1)}, f32[176,128]{1,0:T(8,128)S(1)}, u32[]{:S(2)}, u32[]{:S(2)}) collective-permute-start(f32[176,128]{1,0:T(8,128)S(1)} %slice.4), channel_id=1, source_target_pairs={{0,2},{1,3},{2,0},{3,1},{4,6},{5,7},{6,4},{7,5},{8,10},{9,11},{10,... | collective-permute-start | bytes 270344 | tf_op jit(solution)/shard_map/ppermute | solution.py:287
  7.4 2.5 %collective-permute-done.1.got = f32[176,128]{1,0:T(8,128)S(1)} collective-permute-done((f32[176,128]{1,0:T(8,128)S(1)}, f32[176,128]{1,0:T(8,128)S(1)}, u32[]{:S(2)}, u32[]{:S(2)}) %collective-permute-start.1) | collective-permute-done | bytes 90144 | tf_op jit(solution)/shard_map/ppermute | solution.py:287
  9.9 0.3 features.1
  10.2 2.9 %collective-permute-start.2 = (f32[48,128]{1,0:T(8,128)S(1)}, f32[48,128]{1,0:T(8,128)S(1)}, u32[]{:S(2)}, u32[]{:S(2)}) collective-permute-start(f32[48,128]{1,0:T(8,128)S(1)} %features.1), channel_id=1, source_target_pairs={{0,4},{4,0},{8,12},{12,8},{16,20},{20,16},{24,28},{28,24},{32,36},... | collective-permute-start | bytes 73736 | tf_op jit(solution)/shard_map/ppermute | solution.py:258
  13.1 1.4 %collective-permute-done.2 = f32[48,128]{1,0:T(8,128)S(1)} collective-permute-done((f32[48,128]{1,0:T(8,128)S(1)}, f32[48,128]{1,0:T(8,128)S(1)}, u32[]{:S(2)}, u32[]{:S(2)}) %collective-permute-start.2) | collective-permute-done | bytes 24608 | tf_op jit(solution)/shard_map/ppermute | solution.py:258
  14.5 3.7 %collective-permute-start.3 = (f32[96,128]{1,0:T(8,128)S(1)}, f32[96,128]{1,0:T(8,128)S(1)}, u32[]{:S(2)}, u32[]{:S(2)}) collective-permute-start(f32[96,128]{1,0:T(8,128)S(1)} %pad_maximum_fusion), channel_id=1, source_target_pairs={{0,64},{4,68},{8,72},{12,76},{16,80},{20,84},{24,88},{28,92},{32,9... | collective-permute-start | bytes 147464 | tf_op jit(solution)/shard_map/ppermute | solution.py:258
  18.2 0.7 %collective-permute-start.4 = (f32[96,128]{1,0:T(8,128)S(1)}, f32[96,128]{1,0:T(8,128)S(1)}, u32[]{:S(2)}, u32[]{:S(2)}) collective-permute-start(f32[96,128]{1,0:T(8,128)S(1)} %pad_maximum_fusion), channel_id=1, source_target_pairs={{0,32},{4,36},{8,40},{12,44},{16,48},{20,52},{24,56},{28,60},{32,6... | collective-permute-start | bytes 147464 | tf_op jit(solution)/shard_map/ppermute | solution.py:258
  18.9 1.9 %collective-permute-start.5 = (f32[96,128]{1,0:T(8,128)S(1)}, f32[96,128]{1,0:T(8,128)S(1)}, u32[]{:S(2)}, u32[]{:S(2)}) collective-permute-start(f32[96,128]{1,0:T(8,128)S(1)} %pad_maximum_fusion), channel_id=1, source_target_pairs={{0,96},{4,100},{8,104},{12,108},{16,112},{20,116},{24,120},{28,124... | collective-permute-start | bytes 147464 | tf_op jit(solution)/shard_map/ppermute | solution.py:258
  20.9 0.0 collective-permute-done.3
  20.9 1.8 %collective-permute-done.4 = f32[96,128]{1,0:T(8,128)S(1)} collective-permute-done((f32[96,128]{1,0:T(8,128)S(1)}, f32[96,128]{1,0:T(8,128)S(1)}, u32[]{:S(2)}, u32[]{:S(2)}) %collective-permute-start.4) | collective-permute-done | bytes 49184 | tf_op jit(solution)/shard_map/ppermute | solution.py:258
  22.7 0.0 collective-permute-done.5
  22.7 3.0 %collective-permute-start.6 = (f32[384,128]{1,0:T(8,128)S(1)}, f32[384,128]{1,0:T(8,128)S(1)}, u32[]{:S(2)}, u32[]{:S(2)}) collective-permute-start(f32[384,128]{1,0:T(8,128)S(1)} %get-tuple-element.12), channel_id=1, source_target_pairs={{0,16},{4,20},{8,24},{12,28},{16,0},{20,4},{24,8},{28,12},{32,48},... | collective-permute-start | bytes 589832 | tf_op jit(solution)/shard_map/ppermute | solution.py:258
  25.7 0.4 collective-permute-start.7
  26.1 2.3 %collective-permute-start.8 = (f32[384,128]{1,0:T(8,128)S(1)}, f32[384,128]{1,0:T(8,128)S(1)}, u32[]{:S(2)}, u32[]{:S(2)}) collective-permute-start(f32[384,128]{1,0:T(8,128)S(1)} %get-tuple-element.12), channel_id=1, source_target_pairs={{0,24},{4,28},{8,0},{12,4},{16,8},{20,12},{24,16},{28,20},{32,56},... | collective-permute-start | bytes 589832 | tf_op jit(solution)/shard_map/ppermute | solution.py:258
  28.4 0.4 collective-permute-done.6
  28.9 5.0 %collective-permute-done.7 = f32[384,128]{1,0:T(8,128)S(1)} collective-permute-done((f32[384,128]{1,0:T(8,128)S(1)}, f32[384,128]{1,0:T(8,128)S(1)}, u32[]{:S(2)}, u32[]{:S(2)}) %collective-permute-start.7) | collective-permute-done | bytes 196640 | tf_op jit(solution)/shard_map/ppermute | solution.py:258
  33.9 0.0 collective-permute-done.8
  33.9 0.7 %gram.1 = (f32[136,128]{1,0:T(8,128)S(1)}, bf16[192,1024]{1,0:T(8,128)(2,1)S(1)}, bf16[192,1024]{1,0:T(8,128)(2,1)S(1)}) custom-call(f32[1536,128]{1,0:T(8,128)S(1)} %constant_dynamic-update-slice_fusion.5.tiles), custom_call_target="tpu_custom_call" | custom-call | tf_op jit(solution)/shard_map/gram/pallas_call | solution.py:300
  34.6 2.6 %collective-permute-start.9 = (f32[136,128]{1,0:T(8,128)S(1)}, f32[136,128]{1,0:T(8,128)S(1)}, u32[]{:S(2)}, u32[]{:S(2)}) collective-permute-start(f32[136,128]{1,0:T(8,128)S(1)} %get-tuple-element.9), channel_id=1, source_target_pairs={{0,1},{1,0},{2,3},{3,2},{4,5},{5,4},{6,7},{7,6},{8,9},{9,8},{10,11... | collective-permute-start | bytes 208904 | tf_op jit(solution)/shard_map/ppermute | solution.py:307
  37.2 0.9 %collective-permute-done.9 = f32[136,128]{1,0:T(8,128)S(1)} collective-permute-done((f32[136,128]{1,0:T(8,128)S(1)}, f32[136,128]{1,0:T(8,128)S(1)}, u32[]{:S(2)}, u32[]{:S(2)}) %collective-permute-start.9) | collective-permute-done | bytes 69664 | tf_op jit(solution)/shard_map/ppermute | solution.py:307
  38.1 1.3 %collective-permute-start.10 = (f32[136,128]{1,0:T(8,128)S(1)}, f32[136,128]{1,0:T(8,128)S(1)}, u32[]{:S(2)}, u32[]{:S(2)}) collective-permute-start(f32[136,128]{1,0:T(8,128)S(1)} %add.7.mine), channel_id=1, source_target_pairs={{0,2},{1,3},{2,0},{3,1},{4,6},{5,7},{6,4},{7,5},{8,10},{9,11},{10,... | collective-permute-start | bytes 208904 | tf_op jit(solution)/shard_map/ppermute | solution.py:308
  39.4 1.9 %collective-permute-done.10.got = f32[136,128]{1,0:T(8,128)S(1)} collective-permute-done((f32[136,128]{1,0:T(8,128)S(1)}, f32[136,128]{1,0:T(8,128)S(1)}, u32[]{:S(2)}, u32[]{:S(2)}) %collective-permute-start.10) | collective-permute-done | bytes 69664 | tf_op jit(solution)/shard_map/ppermute | solution.py:308
  41.4 2.1 %solve.1 = (f32[64,1024]{1,0:T(8,128)}, f32[4,16]{1,0:T(4,128)}) custom-call(f32[136,128]{1,0:T(8,128)S(1)} %add.7.mine, f32[136,128]{1,0:T(8,128)S(1)} %collective-permute-done.10.got, bf16[192,1024]{1,0:T(8,128)(2,1)S(1)} %get-tuple-element.10.xh, bf16[192,1024]{1,0:T(8,128)(2,1)S(1)} %get-tuple-element.11.xl), custom_call_target="tpu_custom_call" | custom-call | tf_op jit(solution)/shard_map/solve/pallas_call | solution.py:309
  (12 shorter events, 0.1 us)
Async XLA Ops:
  3.5 2.5 %collective-permute-start = (f32[208,128]{1,0:T(8,128)S(1)}, f32[208,128]{1,0:T(8,128)S(1)}, u32[]{:S(2)}, u32[]{:S(2)}) collective-permute-start(f32[208,128]{1,0:T(8,128)S(1)} %get-tuple-element.8), channel_id=1, source_target_pairs={{0,1},{1,0},{2,3},{3,2},{4,5},{5,4},{6,7},{7,6},{8,9},{9,8},{10,11... | collective-permute-start | bytes 319496 | tf_op jit(solution)/shard_map/ppermute | solution.py:286
  6.0 3.9 %collective-permute-start.1 = (f32[176,128]{1,0:T(8,128)S(1)}, f32[176,128]{1,0:T(8,128)S(1)}, u32[]{:S(2)}, u32[]{:S(2)}) collective-permute-start(f32[176,128]{1,0:T(8,128)S(1)} %slice.4), channel_id=1, source_target_pairs={{0,2},{1,3},{2,0},{3,1},{4,6},{5,7},{6,4},{7,5},{8,10},{9,11},{10,... | collective-permute-start | bytes 270344 | tf_op jit(solution)/shard_map/ppermute | solution.py:287
  10.2 4.2 %collective-permute-start.2 = (f32[48,128]{1,0:T(8,128)S(1)}, f32[48,128]{1,0:T(8,128)S(1)}, u32[]{:S(2)}, u32[]{:S(2)}) collective-permute-start(f32[48,128]{1,0:T(8,128)S(1)} %features.1), channel_id=1, source_target_pairs={{0,4},{4,0},{8,12},{12,8},{16,20},{20,16},{24,28},{28,24},{32,36},... | collective-permute-start | bytes 73736 | tf_op jit(solution)/shard_map/ppermute | solution.py:258
  14.5 6.4 %collective-permute-start.3 = (f32[96,128]{1,0:T(8,128)S(1)}, f32[96,128]{1,0:T(8,128)S(1)}, u32[]{:S(2)}, u32[]{:S(2)}) collective-permute-start(f32[96,128]{1,0:T(8,128)S(1)} %pad_maximum_fusion), channel_id=1, source_target_pairs={{0,64},{4,68},{8,72},{12,76},{16,80},{20,84},{24,88},{28,92},{32,9... | collective-permute-start | bytes 147464 | tf_op jit(solution)/shard_map/ppermute | solution.py:258
  18.2 4.5 %collective-permute-start.4 = (f32[96,128]{1,0:T(8,128)S(1)}, f32[96,128]{1,0:T(8,128)S(1)}, u32[]{:S(2)}, u32[]{:S(2)}) collective-permute-start(f32[96,128]{1,0:T(8,128)S(1)} %pad_maximum_fusion), channel_id=1, source_target_pairs={{0,32},{4,36},{8,40},{12,44},{16,48},{20,52},{24,56},{28,60},{32,6... | collective-permute-start | bytes 147464 | tf_op jit(solution)/shard_map/ppermute | solution.py:258
  18.9 3.8 %collective-permute-start.5 = (f32[96,128]{1,0:T(8,128)S(1)}, f32[96,128]{1,0:T(8,128)S(1)}, u32[]{:S(2)}, u32[]{:S(2)}) collective-permute-start(f32[96,128]{1,0:T(8,128)S(1)} %pad_maximum_fusion), channel_id=1, source_target_pairs={{0,96},{4,100},{8,104},{12,108},{16,112},{20,116},{24,120},{28,124... | collective-permute-start | bytes 147464 | tf_op jit(solution)/shard_map/ppermute | solution.py:258
  22.7 6.1 %collective-permute-start.6 = (f32[384,128]{1,0:T(8,128)S(1)}, f32[384,128]{1,0:T(8,128)S(1)}, u32[]{:S(2)}, u32[]{:S(2)}) collective-permute-start(f32[384,128]{1,0:T(8,128)S(1)} %get-tuple-element.12), channel_id=1, source_target_pairs={{0,16},{4,20},{8,24},{12,28},{16,0},{20,4},{24,8},{28,12},{32,48},... | collective-permute-start | bytes 589832 | tf_op jit(solution)/shard_map/ppermute | solution.py:258
  25.7 8.1 %collective-permute-start.7 = (f32[384,128]{1,0:T(8,128)S(1)}, f32[384,128]{1,0:T(8,128)S(1)}, u32[]{:S(2)}, u32[]{:S(2)}) collective-permute-start(f32[384,128]{1,0:T(8,128)S(1)} %get-tuple-element.12), channel_id=1, source_target_pairs={{0,8},{4,12},{8,16},{12,20},{16,24},{20,28},{24,0},{28,4},{32,40},... | collective-permute-start | bytes 589832 | tf_op jit(solution)/shard_map/ppermute | solution.py:258
  26.1 7.8 %collective-permute-start.8 = (f32[384,128]{1,0:T(8,128)S(1)}, f32[384,128]{1,0:T(8,128)S(1)}, u32[]{:S(2)}, u32[]{:S(2)}) collective-permute-start(f32[384,128]{1,0:T(8,128)S(1)} %get-tuple-element.12), channel_id=1, source_target_pairs={{0,24},{4,28},{8,0},{12,4},{16,8},{20,12},{24,16},{28,20},{32,56},... | collective-permute-start | bytes 589832 | tf_op jit(solution)/shard_map/ppermute | solution.py:258
  34.6 3.5 %collective-permute-start.9 = (f32[136,128]{1,0:T(8,128)S(1)}, f32[136,128]{1,0:T(8,128)S(1)}, u32[]{:S(2)}, u32[]{:S(2)}) collective-permute-start(f32[136,128]{1,0:T(8,128)S(1)} %get-tuple-element.9), channel_id=1, source_target_pairs={{0,1},{1,0},{2,3},{3,2},{4,5},{5,4},{6,7},{7,6},{8,9},{9,8},{10,11... | collective-permute-start | bytes 208904 | tf_op jit(solution)/shard_map/ppermute | solution.py:307
  38.1 3.2 %collective-permute-start.10 = (f32[136,128]{1,0:T(8,128)S(1)}, f32[136,128]{1,0:T(8,128)S(1)}, u32[]{:S(2)}, u32[]{:S(2)}) collective-permute-start(f32[136,128]{1,0:T(8,128)S(1)} %add.7.mine), channel_id=1, source_target_pairs={{0,2},{1,3},{2,0},{3,1},{4,6},{5,7},{6,4},{7,5},{8,10},{9,11},{10,... | collective-permute-start | bytes 208904 | tf_op jit(solution)/shard_map/ppermute | solution.py:308

commit v6 on v5

--- a/solution.py
+++ b/solution.py
@@ -36,12 +36,14 @@
     def load(src, dst):
         return pltpu.make_async_copy(src, dst, sems.at[next(count)])
 
-    groups = [[load(pi, pi_v), load(qa, a_v.at[slots : slots + 16]), load(ta, a_v.at[0:slots])]]
+    groups = [[load(pi, pi_v), load(qa, a_v.at[slots : slots + 16]), load(ta.at[0:128], a_v.at[0:128]),
+               load(ta.at[128:256], a_v.at[128:256])]]
     for lo, hi in zip(bounds[:-1], bounds[1:]):
         cols = pl.ds(lo, hi - lo)
         groups.append([load(po.at[:, cols], po_v.at[:, cols]),
                        load(qg.at[:, cols], g_v.at[slots : slots + 16, cols]),
-                       load(tg.at[:, cols], g_v.at[0:slots, cols])])
+                       load(tg.at[0:128, cols], g_v.at[0:128, cols]),
+                       load(tg.at[128:256, cols], g_v.at[128:256, cols])])
     groups.append([load(tl, tl_s), load(ql, ql_s)])
     for group in groups:
         for c in group:

time: 43.7 us -> 43.7 us (level)
  no operation moved by 1% of the time
where the time goes in v6:
time: 43.7 us; the launch traced here: 43.4 us
  starting transfers between devices  21.7 us (50%)
  waiting for transfers between devices  15 us (34%)
  Pallas kernels  5.93 us (14%)
  between operations  0.72 us (2%)
    ppermute x7, starting transfers between devices, shifts(): pieces[k] = lax.ppermute(array, 'dp', pairs)  14.9 us
    ppermute x7, waiting for transfers between devices, shifts(): pieces[k] = lax.ppermute(array, 'dp', pairs)  8.62 us
    pallas_call x1, Pallas kernels, local(): call(project_kernel, [((208, 128), f32)] * 2, [pl.BlockSpec(memory_space=...  2.86 us
    ppermute x1, starting transfers between devices, local(): part = part + lax.ppermute(part, 'mp', other_core)  2.56 us
    ppermute x1, waiting for transfers between devices, local(): got = lax.ppermute(keep[32:], 'mp', other_chip)  2.55 us
    pallas_call x1, Pallas kernels, local(): call(solve_kernel, [((64, 1024), f32), ((4, 16), f32)], whole(4), [pltpu....  2.06 us
    ppermute x1, waiting for transfers between devices, local(): got = lax.ppermute(part, 'mp', other_chip)  1.95 us
    ppermute x1, starting transfers between devices, local(): keep = keep + lax.ppermute(give, 'mp', other_core)  1.5 us
  transfers between devices with their start and end apart: 11, of which 8 were waited for; matrix products, arithmetic and copies ran while one was open for 0% of the time, Pallas kernels for 0%

profile of v6, /device:TPU:1, one launch (start us, length us, event | category | flops | bytes accessed | tf_op | source)
XLA Modules:
  0.0 43.4 jit_solution(6760939382114265516)
XLA Ops:
  0.6 2.9 %project.1 = (f32[208,128]{1,0:T(8,128)S(1)}, f32[208,128]{1,0:T(8,128)S(1)}) custom-call(s32[4]{0:T(128)} %tl.1, s32[2]{0:T(128)} %ql.1, bf16[256,1024]{1,0:T(8,128)(2,1)} %bitcast.5, bf16[256,3584]{1,0:T(8,128)(2,1)} %bitcast.4, bf16[16,1024]{1,0:T(8,128)(2,1)} %bitcast.7, bf16[16,3584]{1,0:T(8,128)(2,1)} %bitcast.6, bf16[64,1024]{1,0:T(8,128)(2,1)} %pi.1, ...), custom_call_target="tpu_custom_call" | custom-call | tf_op jit(solution)/shard_map/project/pallas_call | solution.py:270
  3.5 1.5 %collective-permute-start = (f32[208,128]{1,0:T(8,128)S(1)}, f32[208,128]{1,0:T(8,128)S(1)}, u32[]{:S(2)}, u32[]{:S(2)}) collective-permute-start(f32[208,128]{1,0:T(8,128)S(1)} %get-tuple-element.8), channel_id=1, source_target_pairs={{0,1},{1,0},{2,3},{3,2},{4,5},{5,4},{6,7},{7,6},{8,9},{9,8},{10,11... | collective-permute-start | bytes 319496 | tf_op jit(solution)/shard_map/ppermute | solution.py:288
  5.0 1.0 %collective-permute-done = f32[208,128]{1,0:T(8,128)S(1)} collective-permute-done((f32[208,128]{1,0:T(8,128)S(1)}, f32[208,128]{1,0:T(8,128)S(1)}, u32[]{:S(2)}, u32[]{:S(2)}) %collective-permute-start) | collective-permute-done | bytes 106528 | tf_op jit(solution)/shard_map/ppermute | solution.py:288
  6.0 1.4 %collective-permute-start.1 = (f32[176,128]{1,0:T(8,128)S(1)}, f32[176,128]{1,0:T(8,128)S(1)}, u32[]{:S(2)}, u32[]{:S(2)}) collective-permute-start(f32[176,128]{1,0:T(8,128)S(1)} %slice.4), channel_id=1, source_target_pairs={{0,2},{1,3},{2,0},{3,1},{4,6},{5,7},{6,4},{7,5},{8,10},{9,11},{10,... | collective-permute-start | bytes 270344 | tf_op jit(solution)/shard_map/ppermute | solution.py:289
  7.4 2.5 %collective-permute-done.1.got = f32[176,128]{1,0:T(8,128)S(1)} collective-permute-done((f32[176,128]{1,0:T(8,128)S(1)}, f32[176,128]{1,0:T(8,128)S(1)}, u32[]{:S(2)}, u32[]{:S(2)}) %collective-permute-start.1) | collective-permute-done | bytes 90144 | tf_op jit(solution)/shard_map/ppermute | solution.py:289
  9.9 0.3 features.1
  10.2 2.9 %collective-permute-start.2 = (f32[48,128]{1,0:T(8,128)S(1)}, f32[48,128]{1,0:T(8,128)S(1)}, u32[]{:S(2)}, u32[]{:S(2)}) collective-permute-start(f32[48,128]{1,0:T(8,128)S(1)} %features.1), channel_id=1, source_target_pairs={{0,4},{4,0},{8,12},{12,8},{16,20},{20,16},{24,28},{28,24},{32,36},... | collective-permute-start | bytes 73736 | tf_op jit(solution)/shard_map/ppermute | solution.py:260
  13.1 1.3 %collective-permute-done.2 = f32[48,128]{1,0:T(8,128)S(1)} collective-permute-done((f32[48,128]{1,0:T(8,128)S(1)}, f32[48,128]{1,0:T(8,128)S(1)}, u32[]{:S(2)}, u32[]{:S(2)}) %collective-permute-start.2) | collective-permute-done | bytes 24608 | tf_op jit(solution)/shard_map/ppermute | solution.py:260
  14.5 3.7 %collective-permute-start.3 = (f32[96,128]{1,0:T(8,128)S(1)}, f32[96,128]{1,0:T(8,128)S(1)}, u32[]{:S(2)}, u32[]{:S(2)}) collective-permute-start(f32[96,128]{1,0:T(8,128)S(1)} %pad_maximum_fusion), channel_id=1, source_target_pairs={{0,64},{4,68},{8,72},{12,76},{16,80},{20,84},{24,88},{28,92},{32,9... | collective-permute-start | bytes 147464 | tf_op jit(solution)/shard_map/ppermute | solution.py:260
  18.2 0.7 %collective-permute-start.4 = (f32[96,128]{1,0:T(8,128)S(1)}, f32[96,128]{1,0:T(8,128)S(1)}, u32[]{:S(2)}, u32[]{:S(2)}) collective-permute-start(f32[96,128]{1,0:T(8,128)S(1)} %pad_maximum_fusion), channel_id=1, source_target_pairs={{0,32},{4,36},{8,40},{12,44},{16,48},{20,52},{24,56},{28,60},{32,6... | collective-permute-start | bytes 147464 | tf_op jit(solution)/shard_map/ppermute | solution.py:260
  18.9 1.9 %collective-permute-start.5 = (f32[96,128]{1,0:T(8,128)S(1)}, f32[96,128]{1,0:T(8,128)S(1)}, u32[]{:S(2)}, u32[]{:S(2)}) collective-permute-start(f32[96,128]{1,0:T(8,128)S(1)} %pad_maximum_fusion), channel_id=1, source_target_pairs={{0,96},{4,100},{8,104},{12,108},{16,112},{20,116},{24,120},{28,124... | collective-permute-start | bytes 147464 | tf_op jit(solution)/shard_map/ppermute | solution.py:260
  20.8 0.0 collective-permute-done.3
  20.9 1.8 %collective-permute-done.4 = f32[96,128]{1,0:T(8,128)S(1)} collective-permute-done((f32[96,128]{1,0:T(8,128)S(1)}, f32[96,128]{1,0:T(8,128)S(1)}, u32[]{:S(2)}, u32[]{:S(2)}) %collective-permute-start.4) | collective-permute-done | bytes 49184 | tf_op jit(solution)/shard_map/ppermute | solution.py:260
  22.7 0.0 collective-permute-done.5
  22.7 3.0 %collective-permute-start.6 = (f32[384,128]{1,0:T(8,128)S(1)}, f32[384,128]{1,0:T(8,128)S(1)}, u32[]{:S(2)}, u32[]{:S(2)}) collective-permute-start(f32[384,128]{1,0:T(8,128)S(1)} %get-tuple-element.12), channel_id=1, source_target_pairs={{0,16},{4,20},{8,24},{12,28},{16,0},{20,4},{24,8},{28,12},{32,48},... | collective-permute-start | bytes 589832 | tf_op jit(solution)/shard_map/ppermute | solution.py:260
  25.7 0.4 collective-permute-start.7
  26.1 2.3 %collective-permute-start.8 = (f32[384,128]{1,0:T(8,128)S(1)}, f32[384,128]{1,0:T(8,128)S(1)}, u32[]{:S(2)}, u32[]{:S(2)}) collective-permute-start(f32[384,128]{1,0:T(8,128)S(1)} %get-tuple-element.12), channel_id=1, source_target_pairs={{0,24},{4,28},{8,0},{12,4},{16,8},{20,12},{24,16},{28,20},{32,56},... | collective-permute-start | bytes 589832 | tf_op jit(solution)/shard_map/ppermute | solution.py:260
  28.4 0.4 collective-permute-done.6
  28.8 5.0 %collective-permute-done.7 = f32[384,128]{1,0:T(8,128)S(1)} collective-permute-done((f32[384,128]{1,0:T(8,128)S(1)}, f32[384,128]{1,0:T(8,128)S(1)}, u32[]{:S(2)}, u32[]{:S(2)}) %collective-permute-start.7) | collective-permute-done | bytes 196640 | tf_op jit(solution)/shard_map/ppermute | solution.py:260
  33.9 0.0 collective-permute-done.8
  33.9 0.7 %gram.1 = (f32[136,128]{1,0:T(8,128)S(1)}, bf16[192,1024]{1,0:T(8,128)(2,1)S(1)}, bf16[192,1024]{1,0:T(8,128)(2,1)S(1)}) custom-call(f32[1536,128]{1,0:T(8,128)S(1)} %constant_dynamic-update-slice_fusion.5.tiles), custom_call_target="tpu_custom_call" | custom-call | tf_op jit(solution)/shard_map/gram/pallas_call | solution.py:302
  34.6 2.6 %collective-permute-start.9 = (f32[136,128]{1,0:T(8,128)S(1)}, f32[136,128]{1,0:T(8,128)S(1)}, u32[]{:S(2)}, u32[]{:S(2)}) collective-permute-start(f32[136,128]{1,0:T(8,128)S(1)} %get-tuple-element.9), channel_id=1, source_target_pairs={{0,1},{1,0},{2,3},{3,2},{4,5},{5,4},{6,7},{7,6},{8,9},{9,8},{10,11... | collective-permute-start | bytes 208904 | tf_op jit(solution)/shard_map/ppermute | solution.py:309
  37.2 0.9 %collective-permute-done.9 = f32[136,128]{1,0:T(8,128)S(1)} collective-permute-done((f32[136,128]{1,0:T(8,128)S(1)}, f32[136,128]{1,0:T(8,128)S(1)}, u32[]{:S(2)}, u32[]{:S(2)}) %collective-permute-start.9) | collective-permute-done | bytes 69664 | tf_op jit(solution)/shard_map/ppermute | solution.py:309
  38.1 1.3 %collective-permute-start.10 = (f32[136,128]{1,0:T(8,128)S(1)}, f32[136,128]{1,0:T(8,128)S(1)}, u32[]{:S(2)}, u32[]{:S(2)}) collective-permute-start(f32[136,128]{1,0:T(8,128)S(1)} %add.7.mine), channel_id=1, source_target_pairs={{0,2},{1,3},{2,0},{3,1},{4,6},{5,7},{6,4},{7,5},{8,10},{9,11},{10,... | collective-permute-start | bytes 208904 | tf_op jit(solution)/shard_map/ppermute | solution.py:310
  39.4 1.9 %collective-permute-done.10.got = f32[136,128]{1,0:T(8,128)S(1)} collective-permute-done((f32[136,128]{1,0:T(8,128)S(1)}, f32[136,128]{1,0:T(8,128)S(1)}, u32[]{:S(2)}, u32[]{:S(2)}) %collective-permute-start.10) | collective-permute-done | bytes 69664 | tf_op jit(solution)/shard_map/ppermute | solution.py:310
  41.3 2.1 %solve.1 = (f32[64,1024]{1,0:T(8,128)}, f32[4,16]{1,0:T(4,128)}) custom-call(f32[136,128]{1,0:T(8,128)S(1)} %add.7.mine, f32[136,128]{1,0:T(8,128)S(1)} %collective-permute-done.10.got, bf16[192,1024]{1,0:T(8,128)(2,1)S(1)} %get-tuple-element.10.xh, bf16[192,1024]{1,0:T(8,128)(2,1)S(1)} %get-tuple-element.11.xl), custom_call_target="tpu_custom_call" | custom-call | tf_op jit(solution)/shard_map/solve/pallas_call | solution.py:311
  (12 shorter events, 0.1 us)
Async XLA Ops:
  3.5 2.5 %collective-permute-start = (f32[208,128]{1,0:T(8,128)S(1)}, f32[208,128]{1,0:T(8,128)S(1)}, u32[]{:S(2)}, u32[]{:S(2)}) collective-permute-start(f32[208,128]{1,0:T(8,128)S(1)} %get-tuple-element.8), channel_id=1, source_target_pairs={{0,1},{1,0},{2,3},{3,2},{4,5},{5,4},{6,7},{7,6},{8,9},{9,8},{10,11... | collective-permute-start | bytes 319496 | tf_op jit(solution)/shard_map/ppermute | solution.py:288
  6.0 3.9 %collective-permute-start.1 = (f32[176,128]{1,0:T(8,128)S(1)}, f32[176,128]{1,0:T(8,128)S(1)}, u32[]{:S(2)}, u32[]{:S(2)}) collective-permute-start(f32[176,128]{1,0:T(8,128)S(1)} %slice.4), channel_id=1, source_target_pairs={{0,2},{1,3},{2,0},{3,1},{4,6},{5,7},{6,4},{7,5},{8,10},{9,11},{10,... | collective-permute-start | bytes 270344 | tf_op jit(solution)/shard_map/ppermute | solution.py:289
  10.2 4.2 %collective-permute-start.2 = (f32[48,128]{1,0:T(8,128)S(1)}, f32[48,128]{1,0:T(8,128)S(1)}, u32[]{:S(2)}, u32[]{:S(2)}) collective-permute-start(f32[48,128]{1,0:T(8,128)S(1)} %features.1), channel_id=1, source_target_pairs={{0,4},{4,0},{8,12},{12,8},{16,20},{20,16},{24,28},{28,24},{32,36},... | collective-permute-start | bytes 73736 | tf_op jit(solution)/shard_map/ppermute | solution.py:260
  14.5 6.4 %collective-permute-start.3 = (f32[96,128]{1,0:T(8,128)S(1)}, f32[96,128]{1,0:T(8,128)S(1)}, u32[]{:S(2)}, u32[]{:S(2)}) collective-permute-start(f32[96,128]{1,0:T(8,128)S(1)} %pad_maximum_fusion), channel_id=1, source_target_pairs={{0,64},{4,68},{8,72},{12,76},{16,80},{20,84},{24,88},{28,92},{32,9... | collective-permute-start | bytes 147464 | tf_op jit(solution)/shard_map/ppermute | solution.py:260
  18.2 4.5 %collective-permute-start.4 = (f32[96,128]{1,0:T(8,128)S(1)}, f32[96,128]{1,0:T(8,128)S(1)}, u32[]{:S(2)}, u32[]{:S(2)}) collective-permute-start(f32[96,128]{1,0:T(8,128)S(1)} %pad_maximum_fusion), channel_id=1, source_target_pairs={{0,32},{4,36},{8,40},{12,44},{16,48},{20,52},{24,56},{28,60},{32,6... | collective-permute-start | bytes 147464 | tf_op jit(solution)/shard_map/ppermute | solution.py:260
  18.9 3.8 %collective-permute-start.5 = (f32[96,128]{1,0:T(8,128)S(1)}, f32[96,128]{1,0:T(8,128)S(1)}, u32[]{:S(2)}, u32[]{:S(2)}) collective-permute-start(f32[96,128]{1,0:T(8,128)S(1)} %pad_maximum_fusion), channel_id=1, source_target_pairs={{0,96},{4,100},{8,104},{12,108},{16,112},{20,116},{24,120},{28,124... | collective-permute-start | bytes 147464 | tf_op jit(solution)/shard_map/ppermute | solution.py:260
  22.7 6.1 %collective-permute-start.6 = (f32[384,128]{1,0:T(8,128)S(1)}, f32[384,128]{1,0:T(8,128)S(1)}, u32[]{:S(2)}, u32[]{:S(2)}) collective-permute-start(f32[384,128]{1,0:T(8,128)S(1)} %get-tuple-element.12), channel_id=1, source_target_pairs={{0,16},{4,20},{8,24},{12,28},{16,0},{20,4},{24,8},{28,12},{32,48},... | collective-permute-start | bytes 589832 | tf_op jit(solution)/shard_map/ppermute | solution.py:260
  25.7 8.1 %collective-permute-start.7 = (f32[384,128]{1,0:T(8,128)S(1)}, f32[384,128]{1,0:T(8,128)S(1)}, u32[]{:S(2)}, u32[]{:S(2)}) collective-permute-start(f32[384,128]{1,0:T(8,128)S(1)} %get-tuple-element.12), channel_id=1, source_target_pairs={{0,8},{4,12},{8,16},{12,20},{16,24},{20,28},{24,0},{28,4},{32,40},... | collective-permute-start | bytes 589832 | tf_op jit(solution)/shard_map/ppermute | solution.py:260
  26.1 7.8 %collective-permute-start.8 = (f32[384,128]{1,0:T(8,128)S(1)}, f32[384,128]{1,0:T(8,128)S(1)}, u32[]{:S(2)}, u32[]{:S(2)}) collective-permute-start(f32[384,128]{1,0:T(8,128)S(1)} %get-tuple-element.12), channel_id=1, source_target_pairs={{0,24},{4,28},{8,0},{12,4},{16,8},{20,12},{24,16},{28,20},{32,56},... | collective-permute-start | bytes 589832 | tf_op jit(solution)/shard_map/ppermute | solution.py:260
  34.6 3.5 %collective-permute-start.9 = (f32[136,128]{1,0:T(8,128)S(1)}, f32[136,128]{1,0:T(8,128)S(1)}, u32[]{:S(2)}, u32[]{:S(2)}) collective-permute-start(f32[136,128]{1,0:T(8,128)S(1)} %get-tuple-element.9), channel_id=1, source_target_pairs={{0,1},{1,0},{2,3},{3,2},{4,5},{5,4},{6,7},{7,6},{8,9},{9,8},{10,11... | collective-permute-start | bytes 208904 | tf_op jit(solution)/shard_map/ppermute | solution.py:309
  38.1 3.2 %collective-permute-start.10 = (f32[136,128]{1,0:T(8,128)S(1)}, f32[136,128]{1,0:T(8,128)S(1)}, u32[]{:S(2)}, u32[]{:S(2)}) collective-permute-start(f32[136,128]{1,0:T(8,128)S(1)} %add.7.mine), channel_id=1, source_target_pairs={{0,2},{1,3},{2,0},{3,1},{4,6},{5,7},{6,4},{7,5},{8,10},{9,11},{10,... | collective-permute-start | bytes 208904 | tf_op jit(solution)/shard_map/ppermute | solution.py:310
